TPU v7x, 256 devices: a whole 4x4x8 slice. The times are simulated.
256 devices in a mesh: rows: 16 (over z, core), cols: 16 (over y, x).
Axes of the slice: x: 4, y: 4, z: 8, core: 2. Of those that a mesh axis runs over, the one named last changes fastest.
Arguments:
- values: float32 [131072, 128], P(('rows', 'cols')), may hold values from -196608 to 196608
- tile_users: int32 [131072, 128], P(('rows', 'cols')), may hold values from 0 to 8191
- tile_items: int32 [131072], P(('rows', 'cols')), may hold values from 0 to 4095
- tile_words: int32 [131072], P(('rows', 'cols')), may hold values from 0 to 4095
- tile_count: int32 [256], P(('rows', 'cols')), may hold values from 128 to 512, as said below
- factor_items: bfloat16 [65536, 128], P(('rows', 'cols'))
- factor_words: bfloat16 [65536, 128], P(('rows', 'cols'))
Outputs:
- factor_users: float32 [131072, 128], P(('rows', 'cols'))
Inputs may be any that keep to these rules, and one draw needn't show every extreme that they name: `tile_count`: 512 is reached on some device in every draw.
All inputs are finite; a program needn't handle non-finite values.
Results may differ from a plain program's by a relative error of at most 0.0003.
Values may be sent and summed in bfloat16 or wider, within the bound.
No kernel may reach another device: no remote copies, remote signals or barrier semaphores. Data moves between devices by JAX's collectives and lax.ppermute only.
A program may use at most 64 MiB of HBM per device.

v0:
```python
import functools

import jax
import jax.numpy as jnp
from jax import lax
from jax.experimental import pallas as pl
from jax.experimental.pallas import tpu as pltpu
from jax.sharding import PartitionSpec as P

RANK = 128
FIBER = 128
TILES = 512
ROWS = 256
OWN = 512
PEERS = 16
USERS = OWN * PEERS
LO = 128
HI = USERS // LO
EXTRA = 16
PARTS = 4
SLICES = 2
PIVOTS = 4
SLICE = RANK // SLICES
SIDE = 4
TILES_OWN = OWN // LO
PART = TILES // PARTS
STEP = 128.0
TOP = 32767.0
NT = (((1,), (1,)), ((), ()))
TN = (((0,), (0,)), ((), ()))
MIB = 1024 * 1024


def in_hbm(shape, dtype, interpret):
    return jax.ShapeDtypeStruct(shape, dtype) if interpret else pltpu.HBM(shape, dtype)


def build_body(v_ref, u_ref, after_ref, high_ref, low_ref, acc_ref, *, block):
    del after_ref
    pitch = block + 1
    hi_iota = lax.broadcasted_iota(jnp.int32, (HI, FIBER), 0)
    lo_iota = lax.broadcasted_iota(jnp.int32, (LO, FIBER), 0)

    def add_block(g, carry):
        at = pl.multiple_of(g * block, block)
        for k in range(block):
            v = v_ref[pl.ds(at + k, 1), :]
            u = u_ref[pl.ds(at + k, 1), :]
            vh = v.astype(jnp.bfloat16).astype(jnp.float32)
            vl = v - vh
            hit = hi_iota == (u >> 7)
            left = jnp.concatenate(
                [jnp.where(hit, vh, 0.0).astype(jnp.bfloat16), jnp.where(hit, vl, 0.0).astype(jnp.bfloat16)], axis=1
            )
            one = jnp.where(lo_iota == (u & 127), 1.0, 0.0).astype(jnp.bfloat16)
            right = jnp.concatenate([one, one], axis=1)
            acc_ref[pl.ds(k, HI, stride=pitch), :] = lax.dot_general(
                left, right, NT, preferred_element_type=jnp.float32
            )
        for h in range(HI):
            weight = acc_ref[pl.ds(h * pitch, block), :]
            high = weight.astype(jnp.bfloat16)
            high_ref[h, pl.ds(at, block), :] = high
            low_ref[h, pl.ds(at, block), :] = (weight - high.astype(jnp.float32)).astype(jnp.bfloat16)
        return carry

    lax.fori_loop(0, PART // block, add_block, 0)


def build_weights(values, users, part, after, block=32, interpret=False):
    return pl.pallas_call(
        functools.partial(build_body, block=block),
        grid=(1,),
        in_specs=[pl.BlockSpec((PART, FIBER), lambda i: (part, 0))] * 2 + [pl.BlockSpec(memory_space=pl.ANY)],
        out_specs=[pl.BlockSpec(memory_space=pltpu.VMEM)] * 2,
        out_shape=[pltpu.VMEM((HI, PART, LO), jnp.bfloat16)] * 2 if not interpret else [jax.ShapeDtypeStruct((HI, PART, LO), jnp.bfloat16)] * 2,
        scratch_shapes=[pltpu.VMEM((HI * (block + 1), LO), jnp.float32)],
        compiler_params=pltpu.CompilerParams(vmem_limit_bytes=20 * MIB),
        cost_estimate=pl.CostEstimate(flops=6 * 10**9, bytes_accessed=20 * 10**6, transcendentals=0),
        name="build_weights",
        interpret=interpret,
    )(values, users, after)


def sources(me):
    z, c = me // 2, me % 2
    way = 1 - 2 * c
    blocks = [(z, c), (z, 1 - c)]
    for k in range(1, 4):
        blocks += [(z - k * way, c), (z - k * way, 1 - c)]
    blocks.append((z - 4 * way, c))
    for k in range(1, 4):
        blocks += [(z + k * way, 1 - c), (z + k * way, c)]
    blocks.append((z + 4 * way, 1 - c))
    return [(chip + 8) % 8 * 2 + core for chip, core in blocks]


def encode(total, store, base):
    most = jnp.max(jnp.abs(total), axis=1, keepdims=True)
    level = jnp.ceil(jnp.log2(jnp.maximum(most, 1e-35)) * STEP + 1.0)
    coded = jnp.round(total * jnp.exp2(level * (-1.0 / STEP)) * TOP).astype(jnp.int32).astype(jnp.int16)
    for i in range(total.shape[1] // LO):
        store[base + i * RANK : base + (i + 1) * RANK, :] = coded[:, i * LO : (i + 1) * LO]
    return jnp.broadcast_to(level, (RANK, RANK)).T[:EXTRA]


def decode(ref, base, tiles, levels):
    level = jnp.broadcast_to(levels, (RANK, RANK)).T
    scale = jnp.exp2(level * (1.0 / STEP)) * (1.0 / TOP)
    return jnp.concatenate(
        [
            ref[base + i * RANK : base + (i + 1) * RANK, :].astype(jnp.int32).astype(jnp.float32) * scale
            for i in range(tiles)
        ],
        axis=1,
    )


def place(me):
    at = lax.axis_index("cols") if me is None else me
    return at // SIDE, at % SIDE


def product_body(*refs, along_x, sizes, me, at):
    first = sizes is not None
    if first:
        item_at, word_at, count = refs[:3]
        pieces = refs[3 : 3 + len(sizes)]
        refs = refs[3 + len(sizes) :]
    else:
        parts_ref, refs = refs[0], refs[1:]
    weights, refs = refs[: 2 * PARTS], refs[2 * PARTS :]
    outs, own_ref = refs[: SIDE - 1], refs[SIDE - 1]
    if first:
        parts_ref, item_ref, word_ref, khatri_ref = refs[SIDE:]
        source = iter(sources(lax.axis_index("rows") if me is None else me))
        for ref, size in zip(pieces, sizes, strict=True):
            for j in range(size):
                row = pl.multiple_of(next(source) * ROWS, ROWS)
                item_ref[pl.ds(row, ROWS), :] = ref[2 * j * ROWS : (2 * j + 1) * ROWS, :].astype(jnp.float32)
                word_ref[pl.ds(row, ROWS), :] = ref[(2 * j + 1) * ROWS : (2 * j + 2) * ROWS, :].astype(jnp.float32)

        def take(g, carry):
            for k in range(16):
                t = g * 16 + k
                khatri_ref[pl.ds(t, 1), :] = item_ref[pl.ds(item_at[t], 1), :] * word_ref[pl.ds(word_at[t], 1), :]
            return carry

        lax.fori_loop(0, TILES // 16, take, 0)
        live = lax.broadcasted_iota(jnp.int32, (TILES, RANK), 0) < count[0]
        khatri = jnp.where(live, khatri_ref[...], 0.0).T
        high = khatri.astype(jnp.bfloat16)
        parts_ref[:RANK, :] = high
        parts_ref[RANK:, :] = (khatri - high.astype(jnp.float32)).astype(jnp.bfloat16)

    y, x = place(at)
    half = 0 if along_x else TILES_OWN // 2
    for k in (1, 2, 3, 0):
        rows = []
        for other in range(SIDE):
            owner = other * SIDE + (x + k) % SIDE if along_x else (y + k) % SIDE * SIDE + other
            base = owner * TILES_OWN + half

            def joined(refs, base=base):
                return jnp.concatenate(
                    [jnp.concatenate([ref[base + i] for ref in refs], axis=0) for i in range(TILES_OWN // 2)], axis=1
                )

            both = jnp.dot(parts_ref[...], joined(weights[:PARTS]), preferred_element_type=jnp.float32)
            rest = jnp.dot(parts_ref[:RANK, :], joined(weights[PARTS:]), preferred_element_type=jnp.float32)
            total = both[:RANK] + (both[RANK:] + rest)
            if k:
                rows.append(encode(total, outs[k - 1], other * (OWN // 2)))
            else:
                own_ref[other] = total
        if k:
            levels = jnp.concatenate([row[:1] for row in rows] + [rows[0][: EXTRA - SIDE]], axis=0)
            outs[k - 1][SIDE * OWN // 2 :, :] = levels.astype(jnp.int32).astype(jnp.int16)


def products(along_x, highs, lows, *, parts=None, pieces=None, scalars=None, me=None, at=None, interpret=False):
    if not interpret:
        highs = [pltpu.with_memory_space_constraint(x, pltpu.VMEM) for x in highs]
        lows = [pltpu.with_memory_space_constraint(x, pltpu.VMEM) for x in lows]
    in_vmem = pl.BlockSpec(memory_space=pltpu.VMEM)
    first = parts is None
    sizes = [x.shape[0] // (2 * ROWS) for x in pieces] if first else None
    operands = (*scalars, *pieces) if first else (parts,)
    in_specs = [pl.BlockSpec(memory_space=pltpu.SMEM)] * 3 + [in_vmem] * len(pieces) if first else [in_vmem]
    out_shape = [jax.ShapeDtypeStruct((SIDE * OWN // 2 + EXTRA, LO), jnp.int16)] * (SIDE - 1)
    out_shape.append(jax.ShapeDtypeStruct((SIDE, RANK, OWN // 2), jnp.float32))
    scratch = []
    if first:
        out_shape.append(jax.ShapeDtypeStruct((2 * RANK, TILES), jnp.bfloat16))
        scratch = [pltpu.VMEM((PEERS * ROWS, RANK), jnp.float32)] * 2 + [pltpu.VMEM((TILES, RANK), jnp.float32)]
    return pl.pallas_call(
        functools.partial(product_body, along_x=along_x, sizes=sizes, me=me, at=at),
        in_specs=in_specs + [in_vmem] * (2 * PARTS),
        out_specs=[in_vmem] * len(out_shape),
        out_shape=out_shape,
        scratch_shapes=scratch,
        compiler_params=pltpu.CompilerParams(vmem_limit_bytes=24 * MIB),
        cost_estimate=pl.CostEstimate(flops=4 * 10**9, bytes_accessed=13 * 10**6, transcendentals=0),
        name="products",
        interpret=interpret,
    )(*operands, *highs, *lows)


def relay_body(own_ref, a_ref, b_ref, c_ref, *refs, along_x, at):
    outs, mine_ref, sum_ref = refs[: SIDE - 1], refs[SIDE - 1], refs[SIDE]
    width = OWN // 2
    for other in range(SIDE):
        total = own_ref[other]
        for ref in (a_ref, b_ref, c_ref):
            levels = ref[SIDE * width :, :].astype(jnp.int32).astype(jnp.float32)
            total = total + decode(ref, other * width, width // LO, levels[other : other + 1])
        sum_ref[other] = total
    y, x = place(at)
    for k in range(SIDE):
        total = sum_ref[((y if along_x else x) + k) % SIDE]
        if k:
            outs[k - 1][width:, :] = encode(total, outs[k - 1], 0).astype(jnp.int32).astype(jnp.int16)
        else:
            mine_ref[...] = total


def relayed(along_x, own, received, at=None, interpret=False):
    in_vmem = pl.BlockSpec(memory_space=pltpu.VMEM)
    return pl.pallas_call(
        functools.partial(relay_body, along_x=along_x, at=at),
        in_specs=[in_vmem] * SIDE,
        out_specs=[in_vmem] * SIDE,
        out_shape=[jax.ShapeDtypeStruct((OWN // 2 + EXTRA, LO), jnp.int16)] * (SIDE - 1)
        + [jax.ShapeDtypeStruct((RANK, OWN // 2), jnp.float32)],
        scratch_shapes=[pltpu.VMEM((SIDE, RANK, OWN // 2), jnp.float32)],
        compiler_params=pltpu.CompilerParams(vmem_limit_bytes=20 * MIB),
        cost_estimate=pl.CostEstimate(flops=2 * 10**9, bytes_accessed=7 * 10**6, transcendentals=0),
        name="relayed",
        interpret=interpret,
    )(own, *received)


def finish_body(*refs):
    inverse_ref, out_ref = refs[2 * SIDE :]
    width = OWN // 2
    sums = []
    for own_ref, *received in (refs[:SIDE], refs[SIDE : 2 * SIDE]):
        total = own_ref[...]
        for ref in received:
            levels = ref[width:, :].astype(jnp.int32).astype(jnp.float32)
            total = total + decode(ref, 0, width // LO, levels[:1])
        sums.append(total)
    out_ref[...] = lax.dot_general(
        jnp.concatenate(sums, axis=1),
        inverse_ref[...],
        TN,
        precision=lax.Precision.HIGHEST,
        preferred_element_type=jnp.float32,
    )


def finish(first, second, inverse, interpret=False):
    in_vmem = pl.BlockSpec(memory_space=pltpu.VMEM)
    return pl.pallas_call(
        finish_body,
        in_specs=[in_vmem] * (2 * SIDE + 1),
        out_specs=in_vmem,
        out_shape=jax.ShapeDtypeStruct((OWN, RANK), jnp.float32),
        compiler_params=pltpu.CompilerParams(vmem_limit_bytes=20 * MIB),
        name="finish",
        interpret=interpret,
    )(*first, *second, inverse)


def gram_body(*refs, me):
    pieces, out_ref, gram_ref = refs[:-2], refs[-2], refs[-1]
    mine = (lax.axis_index("rows") if me is None else me) % SLICES
    for i in range(2):
        x = jnp.concatenate(
            [ref[at : at + ROWS, :] for ref in pieces for at in range(i * ROWS, ref.shape[0], 2 * ROWS)], axis=0
        )
        gram_ref[...] = lax.dot_general(x, x, TN, preferred_element_type=jnp.float32)
        out_ref[i] = gram_ref[pl.ds(pl.multiple_of(mine * SLICE, SLICE), SLICE), :]


def partial_grams(pieces, me=None, interpret=False):
    return pl.pallas_call(
        functools.partial(gram_body, me=me),
        in_specs=[pl.BlockSpec(memory_space=pltpu.VMEM)] * len(pieces),
        out_specs=pl.BlockSpec(memory_space=pltpu.VMEM),
        out_shape=jax.ShapeDtypeStruct((2, SLICE, RANK), jnp.float32),
        scratch_shapes=[pltpu.VMEM((RANK, RANK), jnp.float32)],
        compiler_params=pltpu.CompilerParams(vmem_limit_bytes=20 * MIB),
        cost_estimate=pl.CostEstimate(flops=10**9, bytes_accessed=3 * 10**6, transcendentals=0),
        name="partial_grams",
        interpret=interpret,
    )(*pieces)


def fold_body(after_ref, a_ref, b_ref, out_ref, *, multiply):
    del after_ref
    if multiply:
        out_ref[...] = (a_ref[0] + b_ref[0]) * (a_ref[1] + b_ref[1])
    else:
        out_ref[...] = a_ref[...] + b_ref[...]


def folded(after, a, b, multiply=False, interpret=False):
    in_vmem = pl.BlockSpec(memory_space=pltpu.VMEM)
    return pl.pallas_call(
        functools.partial(fold_body, multiply=multiply),
        in_specs=[pl.BlockSpec(memory_space=pl.ANY), in_vmem, in_vmem],
        out_specs=in_vmem,
        out_shape=jax.ShapeDtypeStruct(a.shape[1:] if multiply else a.shape, jnp.float32),
        compiler_params=pltpu.CompilerParams(vmem_limit_bytes=20 * MIB),
        name="folded",
        interpret=interpret,
    )(after, a, b)


def inverse_body(mine_ref, other_ref, out_ref, gram_ref, *, me):
    core = (lax.axis_index("rows") if me is None else me) % 2
    gram_ref[pl.ds(pl.multiple_of(core * SLICE, SLICE), SLICE), :] = mine_ref[...]
    gram_ref[pl.ds(pl.multiple_of((1 - core) * SLICE, SLICE), SLICE), :] = other_ref[...]
    a = gram_ref[...]
    lane = lax.broadcasted_iota(jnp.int32, (1, RANK), 1)
    sublane = lax.broadcasted_iota(jnp.int32, (RANK, 1), 0)
    for k in range(0, RANK, PIVOTS):
        order = range(PIVOTS)
        rows = [a[k + i : k + i + 1, :] for i in order]
        block = [[jnp.broadcast_to(rows[i][:, k + j : k + j + 1], (1, RANK)) for j in order] for i in order]
        columns = [a[:, k + i : k + i + 1] for i in order]
        inside = (lane >= k) & (lane < k + PIVOTS)
        rows = [jnp.where(inside, jnp.where(lane == k + i, 1.0, 0.0), rows[i]) for i in order]
        for j in order:
            scale = 1.0 / block[j][j]
            for i in order:
                if i != j:
                    ratio = block[i][j] * scale
                    rows[i] = rows[i] - ratio * rows[j]
                    for n in range(j + 1, PIVOTS):
                        block[i][n] = block[i][n] - ratio * block[j][n]
            rows[j] = rows[j] * scale
            for n in range(j + 1, PIVOTS):
                block[j][n] = block[j][n] * scale
        a = jnp.where(inside, 0.0, a)
        for i in order:
            a = a - columns[i] * rows[i]
        for i in order:
            a = jnp.where(sublane == k + i, rows[i], a)
    out_ref[...] = a


def inverted(mine, other, me=None, interpret=False):
    in_vmem = pl.BlockSpec(memory_space=pltpu.VMEM)
    return pl.pallas_call(
        functools.partial(inverse_body, me=me),
        in_specs=[in_vmem, in_vmem],
        out_specs=in_vmem,
        out_shape=jax.ShapeDtypeStruct((RANK, RANK), jnp.float32),
        scratch_shapes=[pltpu.VMEM((RANK, RANK), jnp.float32)],
        compiler_params=pltpu.CompilerParams(vmem_limit_bytes=20 * MIB),
        cost_estimate=pl.CostEstimate(flops=4 * 10**9, bytes_accessed=15 * 10**6, transcendentals=0),
        name="inverted",
        interpret=interpret,
    )(mine, other)


def swapped(bits):
    return [(i, i ^ bits) for i in range(PEERS)]


def along(xs, along_x):
    def moved(k):
        dy, dx = (0, k) if along_x else (k, 0)
        return [(SIDE * y + x, SIDE * ((y + dy) % SIDE) + (x + dx) % SIDE) for y in range(SIDE) for x in range(SIDE)]

    last, first, second = (lax.ppermute(xs[k - 1], "cols", moved(k)) for k in (2, 1, 3))
    return [first, last, second]


def on_device(values, tile_users, tile_items, tile_words, tile_count, factor_items, factor_words):
    across = swapped(1)
    around = [(2 * z, 2 * ((z + 1) % 8)) for z in range(8)] + [(2 * z + 1, 2 * ((z + 7) % 8) + 1) for z in range(8)]
    after = lax.optimization_barrier
    others = [lax.ppermute(x, "rows", across) for x in (factor_items, factor_words)]
    found = [jnp.concatenate([factor_items, factor_words, *others], axis=0)]
    highs, lows = [], []
    grams = partial_grams(found)
    more = lax.ppermute(grams, "cols", swapped(1))
    for step in range(4):
        arriving = lax.ppermute(found[-1] if step < 3 else found[-1][: 2 * ROWS], "rows", around)
        high, low = build_weights(values, tile_users, step, found[-1])
        if step == 0:
            grams = folded(found[-1], grams, more)
            arriving, low, grams = after((arriving, low, grams))
            more = lax.ppermute(grams, "cols", swapped(2))
        else:
            grams = folded(found[-1], grams, more)
            more = lax.ppermute(grams, *(("cols", swapped(2 << step)) if step < 3 else ("rows", swapped(2))))
            arriving, low, more = after((arriving, low, more))
        highs.append(high)
        lows.append(low)
        found.append(arriving)
    pieces = found + [lax.ppermute(x, "rows", across) for x in found[1:]]
    scalars = (tile_items, tile_words, tile_count)
    *out, own_a, parts = products(True, highs, lows, pieces=pieces, scalars=scalars)
    in_a = along(out, True)
    *out, own_b = products(False, highs, lows, parts=parts)
    in_b = along(out, False)
    grams = folded(own_b, grams, more)
    more = lax.ppermute(grams, "rows", swapped(4))
    own_a, more = after((own_a, more))
    *out, own_a = relayed(True, own_a, in_a)
    end_a = along(out, False)
    grams = folded(own_a, grams, more)
    more = lax.ppermute(grams, "rows", swapped(8))
    *out, own_b = relayed(False, own_b, in_b)
    end_b = along(out, True)
    grams = folded(own_b, grams, more, multiply=True)
    inverse = inverted(grams, lax.ppermute(grams, "rows", across))
    return finish((own_a, *end_a), (own_b, *end_b), inverse)


def solution(mesh):
    placed = (
        P(("rows", "cols"), None),
        P(("rows", "cols"), None),
        P(("rows", "cols")),
        P(("rows", "cols")),
        P(("rows", "cols")),
        P(("rows", "cols"), None),
        P(("rows", "cols"), None),
    )
    return jax.shard_map(
        on_device, mesh=mesh, in_specs=placed, out_specs=P(("rows", "cols"), None), check_vma=False
    )
```

profile of v0, /device:TPU:32, one launch (start us, length us, event | category | flops | bytes accessed | tf_op | source)
XLA Modules:
  0.0 85.9 jit_solution(17644362982195490410)
XLA Ops:
  2.6 2.0 %collective-permute-start.2 = (bf16[1024,128]{1,0:T(8,128)(2,1)S(1)}, bf16[1024,128]{1,0:T(8,128)(2,1)S(1)}, u32[]{:S(2)}, u32[]{:S(2)}) collective-permute-start(bf16[1024,128]{1,0:T(8,128)(2,1)S(1)} %constant_dynamic-update-slice_fusion.after_ref.refs_0_.refs_3_), channel_id=1, source_target_pairs={{0,32},{32,64},{64,96},{96,128},{128,160},{160,192},{192,224},{224... | collective-permute-start | bytes 786440 | tf_op jit(solution)/shard_map/ppermute | solution.py:392
  4.5 1.5 %collective-permute-start.3 = (f32[2,64,128]{2,1,0:T(8,128)S(1)}, f32[2,64,128]{2,1,0:T(8,128)S(1)}, u32[]{:S(2)}, u32[]{:S(2)}) collective-permute-start(f32[2,64,128]{2,1,0:T(8,128)S(1)} %partial_grams.1.a_ref), channel_id=1, source_target_pairs={{0,1},{1,0},{2,3},{3,2},{4,5},{5,4},{6,7},{7,6},{8,9},{9,8},{10,11... | collective-permute-start | bytes 196616 | tf_op jit(solution)/shard_map/ppermute | solution.py:390
  6.0 3.8 %build_weights.4 = (bf16[64,128,128]{2,1,0:T(8,128)(2,1)S(1)}, bf16[64,128,128]{2,1,0:T(8,128)(2,1)S(1)}) custom-call(f32[512,128]{1,0:T(8,128)S(1)} %copy-done.2, s32[512,128]{1,0:T(8,128)S(1)} %copy-done.3, bf16[1024,128]{1,0:T(8,128)(2,1)S(1)} %constant_dynamic-update-slice_fusion.after_ref.refs_0_.refs_3_), custom_call_target="tpu_custom_call" | custom-call | flops 6000000000 | bytes 20000000 | tf_op jit(solution)/shard_map/build_weights/pallas_call | solution.py:71
  9.9 2.8 %collective-permute-start.5 = (f32[2,64,128]{2,1,0:T(8,128)S(1)}, f32[2,64,128]{2,1,0:T(8,128)S(1)}, u32[]{:S(2)}, u32[]{:S(2)}) collective-permute-start(f32[2,64,128]{2,1,0:T(8,128)S(1)} %folded.7.a_ref), channel_id=1, source_target_pairs={{0,2},{1,3},{2,0},{3,1},{4,6},{5,7},{6,4},{7,5},{8,10},{9,11},{10,... | collective-permute-start | bytes 196616 | tf_op jit(solution)/shard_map/ppermute | solution.py:397
  12.7 1.9 %collective-permute-start.4 = (bf16[1024,128]{1,0:T(8,128)(2,1)S(1)}, bf16[1024,128]{1,0:T(8,128)(2,1)S(1)}, u32[]{:S(2)}, u32[]{:S(2)}) collective-permute-start(bf16[1024,128]{1,0:T(8,128)(2,1)S(1)} %collective-permute-done.2.after_ref.refs_4_), channel_id=1, source_target_pairs={{0,32},{32,64},{64,96},{96,128},{128,160},{160,192},{192,224},{224... | collective-permute-start | bytes 786440 | tf_op jit(solution)/shard_map/ppermute | solution.py:392
  15.8 1.7 %collective-permute-start.6 = (f32[2,64,128]{2,1,0:T(8,128)S(1)}, f32[2,64,128]{2,1,0:T(8,128)S(1)}, u32[]{:S(2)}, u32[]{:S(2)}) collective-permute-start(f32[2,64,128]{2,1,0:T(8,128)S(1)} %folded.8.a_ref), channel_id=1, source_target_pairs={{0,4},{1,5},{2,6},{3,7},{4,0},{5,1},{6,2},{7,3},{8,12},{9,13},{10,... | collective-permute-start | bytes 196616 | tf_op jit(solution)/shard_map/ppermute | solution.py:400
  17.4 3.7 %build_weights.5 = (bf16[64,128,128]{2,1,0:T(8,128)(2,1)S(1)}, bf16[64,128,128]{2,1,0:T(8,128)(2,1)S(1)}) custom-call(f32[512,128]{1,0:T(8,128)S(1)} %copy-done.2, s32[512,128]{1,0:T(8,128)S(1)} %copy-done.3, bf16[1024,128]{1,0:T(8,128)(2,1)S(1)} %collective-permute-done.2.after_ref.refs_4_), custom_call_target="tpu_custom_call" | custom-call | flops 6000000000 | bytes 20000000 | tf_op jit(solution)/shard_map/build_weights/pallas_call | solution.py:71
  21.4 1.9 %collective-permute-start.7 = (bf16[1024,128]{1,0:T(8,128)(2,1)S(1)}, bf16[1024,128]{1,0:T(8,128)(2,1)S(1)}, u32[]{:S(2)}, u32[]{:S(2)}) collective-permute-start(bf16[1024,128]{1,0:T(8,128)(2,1)S(1)} %collective-permute-done.4.after_ref.refs_5_), channel_id=1, source_target_pairs={{0,32},{32,64},{64,96},{96,128},{128,160},{160,192},{192,224},{224... | collective-permute-start | bytes 786440 | tf_op jit(solution)/shard_map/ppermute | solution.py:392
  23.4 3.0 %collective-permute-start.8 = (f32[2,64,128]{2,1,0:T(8,128)S(1)}, f32[2,64,128]{2,1,0:T(8,128)S(1)}, u32[]{:S(2)}, u32[]{:S(2)}) collective-permute-start(f32[2,64,128]{2,1,0:T(8,128)S(1)} %folded.9.a_ref), channel_id=1, source_target_pairs={{0,8},{1,9},{2,10},{3,11},{4,12},{5,13},{6,14},{7,15},{8,0},{9,1},... | collective-permute-start | bytes 196616 | tf_op jit(solution)/shard_map/ppermute | solution.py:400
  26.3 3.8 %build_weights.6 = (bf16[64,128,128]{2,1,0:T(8,128)(2,1)S(1)}, bf16[64,128,128]{2,1,0:T(8,128)(2,1)S(1)}) custom-call(f32[512,128]{1,0:T(8,128)S(1)} %copy-done.2, s32[512,128]{1,0:T(8,128)S(1)} %copy-done.3, bf16[1024,128]{1,0:T(8,128)(2,1)S(1)} %collective-permute-done.4.after_ref.refs_5_), custom_call_target="tpu_custom_call" | custom-call | flops 6000000000 | bytes 20000000 | tf_op jit(solution)/shard_map/build_weights/pallas_call | solution.py:71
  30.2 1.3 %collective-permute-start.13 = (bf16[1024,128]{1,0:T(8,128)(2,1)S(1)}, bf16[1024,128]{1,0:T(8,128)(2,1)S(1)}, u32[]{:S(2)}, u32[]{:S(2)}) collective-permute-start(bf16[1024,128]{1,0:T(8,128)(2,1)S(1)} %collective-permute-done.7.after_ref.refs_6_), channel_id=1, source_target_pairs={{0,16},{16,0},{32,48},{48,32},{64,80},{80,64},{96,112},{112,96},{1... | collective-permute-start | bytes 786440 | tf_op jit(solution)/shard_map/ppermute | solution.py:405
  31.5 1.7 %collective-permute-start.10 = (f32[2,64,128]{2,1,0:T(8,128)S(1)}, f32[2,64,128]{2,1,0:T(8,128)S(1)}, u32[]{:S(2)}, u32[]{:S(2)}) collective-permute-start(f32[2,64,128]{2,1,0:T(8,128)S(1)} %folded.10.a_ref), channel_id=1, source_target_pairs={{0,32},{16,48},{32,0},{48,16},{64,96},{80,112},{96,64},{112,80},{1... | collective-permute-start | bytes 196616 | tf_op jit(solution)/shard_map/ppermute | solution.py:400
  33.2 2.4 %collective-permute-start.9 = (bf16[512,128]{1,0:T(8,128)(2,1)S(1)}, bf16[512,128]{1,0:T(8,128)(2,1)S(1)}, u32[]{:S(2)}, u32[]{:S(2)}) collective-permute-start(bf16[512,128]{1,0:T(8,128)(2,1)S(1)} %slice.3), channel_id=1, source_target_pairs={{0,32},{32,64},{64,96},{96,128},{128,160},{160,192},{192,224},{224... | collective-permute-start | bytes 393224 | tf_op jit(solution)/shard_map/ppermute | solution.py:392
  35.6 3.8 %build_weights.7 = (bf16[64,128,128]{2,1,0:T(8,128)(2,1)S(1)}, bf16[64,128,128]{2,1,0:T(8,128)(2,1)S(1)}) custom-call(f32[512,128]{1,0:T(8,128)S(1)} %copy-done.2, s32[512,128]{1,0:T(8,128)S(1)} %copy-done.3, bf16[1024,128]{1,0:T(8,128)(2,1)S(1)} %collective-permute-done.7.after_ref.refs_6_), custom_call_target="tpu_custom_call" | custom-call | flops 6000000000 | bytes 20000000 | tf_op jit(solution)/shard_map/build_weights/pallas_call | solution.py:71
  41.1 3.7 %products.2 = (s16[1040,128]{1,0:T(8,128)(2,1)S(1)}, s16[1040,128]{1,0:T(8,128)(2,1)S(1)}, s16[1040,128]{1,0:T(8,128)(2,1)S(1)}, f32[4,128,256]{2,1,0:T(8,128)S(1)}, bf16[256,512]{1,0:T(8,128)(2,1)S(1)}) custom-call(s32[512]{0:T(512)S(1)} %copy-done, s32[512]{0:T(512)S(1)} %copy-done.1, s32[1]{0:T(128)S(6)} %copy.11.refs_2_, ...), custom_call_target="tpu_custom_call" | custom-call | flops 4000000000 | bytes 13000000 | tf_op jit(solution)/shard_map/products/pallas_call | solution.py:196
  44.7 1.6 %collective-permute-start.16 = (s16[1040,128]{1,0:T(8,128)(2,1)S(1)}, s16[1040,128]{1,0:T(8,128)(2,1)S(1)}, u32[]{:S(2)}, u32[]{:S(2)}) collective-permute-start(s16[1040,128]{1,0:T(8,128)(2,1)S(1)} %get-tuple-element.68), channel_id=1, source_target_pairs={{0,1},{1,2},{2,3},{3,0},{4,5},{5,6},{6,7},{7,4},{8,9},{9,10},{10,1... | collective-permute-start | bytes 798728 | tf_op jit(solution)/shard_map/ppermute | solution.py:378
  46.3 2.7 %collective-permute-start.17 = (s16[1040,128]{1,0:T(8,128)(2,1)S(1)}, s16[1040,128]{1,0:T(8,128)(2,1)S(1)}, u32[]{:S(2)}, u32[]{:S(2)}) collective-permute-start(s16[1040,128]{1,0:T(8,128)(2,1)S(1)} %get-tuple-element.69), channel_id=1, source_target_pairs={{0,2},{1,3},{2,0},{3,1},{4,6},{5,7},{6,4},{7,5},{8,10},{9,11},{10,... | collective-permute-start | bytes 798728 | tf_op jit(solution)/shard_map/ppermute | solution.py:378
  49.0 1.4 %collective-permute-start.18 = (s16[1040,128]{1,0:T(8,128)(2,1)S(1)}, s16[1040,128]{1,0:T(8,128)(2,1)S(1)}, u32[]{:S(2)}, u32[]{:S(2)}) collective-permute-start(s16[1040,128]{1,0:T(8,128)(2,1)S(1)} %get-tuple-element.70), channel_id=1, source_target_pairs={{0,3},{1,0},{2,1},{3,2},{4,7},{5,4},{6,5},{7,6},{8,11},{9,8},{10,9... | collective-permute-start | bytes 798728 | tf_op jit(solution)/shard_map/ppermute | solution.py:378
  50.5 1.8 %products.3 = (s16[1040,128]{1,0:T(8,128)(2,1)S(1)}, s16[1040,128]{1,0:T(8,128)(2,1)S(1)}, s16[1040,128]{1,0:T(8,128)(2,1)S(1)}, f32[4,128,256]{2,1,0:T(8,128)S(1)}) custom-call(bf16[256,512]{1,0:T(8,128)(2,1)S(1)} %get-tuple-element.64.refs_0_, bf16[64,128,128]{2,1,0:T(8,128)(2,1)S(1)} %get-tuple-element.55.refs_12_.refs_1_, ...), custom_call_target="tpu_custom_call" | custom-call | flops 4000000000 | bytes 13000000 | tf_op jit(solution)/shard_map/products/pallas_call | solution.py:196
  52.3 1.4 %collective-permute-start.15 = (f32[2,64,128]{2,1,0:T(8,128)S(1)}, f32[2,64,128]{2,1,0:T(8,128)S(1)}, u32[]{:S(2)}, u32[]{:S(2)}) collective-permute-start(f32[2,64,128]{2,1,0:T(8,128)S(1)} %folded.11.a_ref), channel_id=1, source_target_pairs={{0,64},{16,80},{32,96},{48,112},{64,0},{80,16},{96,32},{112,48},{1... | collective-permute-start | bytes 196616 | tf_op jit(solution)/shard_map/ppermute | solution.py:412
  53.9 3.7 %collective-permute-done.15.b_ref = f32[2,64,128]{2,1,0:T(8,128)S(1)} collective-permute-done((f32[2,64,128]{2,1,0:T(8,128)S(1)}, f32[2,64,128]{2,1,0:T(8,128)S(1)}, u32[]{:S(2)}, u32[]{:S(2)}) %collective-permute-start.15) | collective-permute-done | bytes 65568 | tf_op jit(solution)/shard_map/ppermute | solution.py:412
  57.6 1.9 %collective-permute-start.23 = (s16[1040,128]{1,0:T(8,128)(2,1)S(1)}, s16[1040,128]{1,0:T(8,128)(2,1)S(1)}, u32[]{:S(2)}, u32[]{:S(2)}) collective-permute-start(s16[1040,128]{1,0:T(8,128)(2,1)S(1)} %get-tuple-element.76), channel_id=1, source_target_pairs={{0,8},{1,9},{2,10},{3,11},{4,12},{5,13},{6,14},{7,15},{8,0},{9,1},... | collective-permute-start | bytes 798728 | tf_op jit(solution)/shard_map/ppermute | solution.py:378
  61.7 2.0 %collective-permute-start.28 = (f32[2,64,128]{2,1,0:T(8,128)S(1)}, f32[2,64,128]{2,1,0:T(8,128)S(1)}, u32[]{:S(2)}, u32[]{:S(2)}) collective-permute-start(f32[2,64,128]{2,1,0:T(8,128)S(1)} %folded.12.a_ref), channel_id=1, source_target_pairs={{0,128},{16,144},{32,160},{48,176},{64,192},{80,208},{96,224},{112... | collective-permute-start | bytes 196616 | tf_op jit(solution)/shard_map/ppermute | solution.py:417
  63.8 4.2 %collective-permute-done.22.a_ref = s16[1040,128]{1,0:T(8,128)(2,1)S(1)} collective-permute-done((s16[1040,128]{1,0:T(8,128)(2,1)S(1)}, s16[1040,128]{1,0:T(8,128)(2,1)S(1)}, u32[]{:S(2)}, u32[]{:S(2)}) %collective-permute-start.22) | collective-permute-done | bytes 266272 | tf_op jit(solution)/shard_map/ppermute | solution.py:378
  67.9 2.0 %collective-permute-done.24.c_ref = s16[1040,128]{1,0:T(8,128)(2,1)S(1)} collective-permute-done((s16[1040,128]{1,0:T(8,128)(2,1)S(1)}, s16[1040,128]{1,0:T(8,128)(2,1)S(1)}, u32[]{:S(2)}, u32[]{:S(2)}) %collective-permute-start.24) | collective-permute-done | bytes 266272 | tf_op jit(solution)/shard_map/ppermute | solution.py:378
  71.4 1.4 %collective-permute-start.26 = (s16[272,128]{1,0:T(8,128)(2,1)S(1)}, s16[272,128]{1,0:T(8,128)(2,1)S(1)}, u32[]{:S(2)}, u32[]{:S(2)}) collective-permute-start(s16[272,128]{1,0:T(8,128)(2,1)S(1)} %get-tuple-element.80), channel_id=1, source_target_pairs={{0,2},{1,3},{2,0},{3,1},{4,6},{5,7},{6,4},{7,5},{8,10},{9,11},{10,... | collective-permute-start | bytes 208904 | tf_op jit(solution)/shard_map/ppermute | solution.py:378
  72.9 1.4 %collective-permute-start.27 = (s16[272,128]{1,0:T(8,128)(2,1)S(1)}, s16[272,128]{1,0:T(8,128)(2,1)S(1)}, u32[]{:S(2)}, u32[]{:S(2)}) collective-permute-start(s16[272,128]{1,0:T(8,128)(2,1)S(1)} %get-tuple-element.81), channel_id=1, source_target_pairs={{0,3},{1,0},{2,1},{3,2},{4,7},{5,4},{6,5},{7,6},{8,11},{9,8},{10,9... | collective-permute-start | bytes 208904 | tf_op jit(solution)/shard_map/ppermute | solution.py:378
  74.3 1.6 %collective-permute-start.19 = (s16[272,128]{1,0:T(8,128)(2,1)S(1)}, s16[272,128]{1,0:T(8,128)(2,1)S(1)}, u32[]{:S(2)}, u32[]{:S(2)}) collective-permute-start(s16[272,128]{1,0:T(8,128)(2,1)S(1)} %get-tuple-element.72), channel_id=1, source_target_pairs={{0,4},{1,5},{2,6},{3,7},{4,8},{5,9},{6,10},{7,11},{8,12},{9,13},{1... | collective-permute-start | bytes 208904 | tf_op jit(solution)/shard_map/ppermute | solution.py:378
  76.1 2.3 %collective-permute-start.20 = (s16[272,128]{1,0:T(8,128)(2,1)S(1)}, s16[272,128]{1,0:T(8,128)(2,1)S(1)}, u32[]{:S(2)}, u32[]{:S(2)}) collective-permute-start(s16[272,128]{1,0:T(8,128)(2,1)S(1)} %get-tuple-element.73), channel_id=1, source_target_pairs={{0,8},{1,9},{2,10},{3,11},{4,12},{5,13},{6,14},{7,15},{8,0},{9,1},... | collective-permute-start | bytes 208904 | tf_op jit(solution)/shard_map/ppermute | solution.py:378
  78.4 1.9 %collective-permute-start.21 = (s16[272,128]{1,0:T(8,128)(2,1)S(1)}, s16[272,128]{1,0:T(8,128)(2,1)S(1)}, u32[]{:S(2)}, u32[]{:S(2)}) collective-permute-start(s16[272,128]{1,0:T(8,128)(2,1)S(1)} %get-tuple-element.74), channel_id=1, source_target_pairs={{0,12},{1,13},{2,14},{3,15},{4,0},{5,1},{6,2},{7,3},{8,4},{9,5},{1... | collective-permute-start | bytes 208904 | tf_op jit(solution)/shard_map/ppermute | solution.py:378
  80.3 4.3 %inverted.1.refs_8_ = f32[128,128]{1,0:T(8,128)S(1)} custom-call(f32[64,128]{1,0:T(8,128)S(1)} %folded.13.mine_ref, f32[64,128]{1,0:T(8,128)S(1)} %collective-permute-done.29.other_ref), custom_call_target="tpu_custom_call" | custom-call | flops 4000000000 | bytes 15000000 | tf_op jit(solution)/shard_map/inverted/pallas_call | solution.py:356
  84.6 1.3 %finish.1 = f32[512,128]{1,0:T(8,128)} custom-call(f32[128,256]{1,0:T(8,128)S(1)} %get-tuple-element.71.after_ref.refs_0_, s16[272,128]{1,0:T(8,128)(2,1)S(1)} %collective-permute-done.19.refs_1_, s16[272,128]{1,0:T(8,128)(2,1)S(1)} %collective-permute-done.20.refs_2_, s16[272,128]{1,0:T(8,128)(2,1)S(1)} %collective-permute-done.21.refs_3_, ...), custom_call_target="tpu_custom_call" | custom-call | tf_op jit(solution)/shard_map/finish/pallas_call | solution.py:264
  (59 shorter events, 9.0 us)
Async XLA Ops:
  0.0 2.2 %collective-permute-start = (bf16[256,128]{1,0:T(8,128)(2,1)}, bf16[256,128]{1,0:T(8,128)(2,1)S(1)}, u32[]{:S(2)}, u32[]{:S(2)}) collective-permute-start(bf16[256,128]{1,0:T(8,128)(2,1)} %param.12), channel_id=1, source_target_pairs={{0,16},{16,0},{32,48},{48,32},{64,80},{80,64},{96,112},{112,96},{1... | collective-permute-start | bytes 196616 | tf_op jit(solution)/shard_map/ppermute | solution.py:386
  0.0 2.2 %collective-permute-start.1 = (bf16[256,128]{1,0:T(8,128)(2,1)}, bf16[256,128]{1,0:T(8,128)(2,1)S(1)}, u32[]{:S(2)}, u32[]{:S(2)}) collective-permute-start(bf16[256,128]{1,0:T(8,128)(2,1)} %param.13), channel_id=1, source_target_pairs={{0,16},{16,0},{32,48},{48,32},{64,80},{80,64},{96,112},{112,96},{1... | collective-permute-start | bytes 196616 | tf_op jit(solution)/shard_map/ppermute | solution.py:386
  2.6 7.4 %collective-permute-start.2 = (bf16[1024,128]{1,0:T(8,128)(2,1)S(1)}, bf16[1024,128]{1,0:T(8,128)(2,1)S(1)}, u32[]{:S(2)}, u32[]{:S(2)}) collective-permute-start(bf16[1024,128]{1,0:T(8,128)(2,1)S(1)} %constant_dynamic-update-slice_fusion.after_ref.refs_0_.refs_3_), channel_id=1, source_target_pairs={{0,32},{32,64},{64,96},{96,128},{128,160},{160,192},{192,224},{224... | collective-permute-start | bytes 786440 | tf_op jit(solution)/shard_map/ppermute | solution.py:392
  4.5 5.3 %collective-permute-start.3 = (f32[2,64,128]{2,1,0:T(8,128)S(1)}, f32[2,64,128]{2,1,0:T(8,128)S(1)}, u32[]{:S(2)}, u32[]{:S(2)}) collective-permute-start(f32[2,64,128]{2,1,0:T(8,128)S(1)} %partial_grams.1.a_ref), channel_id=1, source_target_pairs={{0,1},{1,0},{2,3},{3,2},{4,5},{5,4},{6,7},{7,6},{8,9},{9,8},{10,11... | collective-permute-start | bytes 196616 | tf_op jit(solution)/shard_map/ppermute | solution.py:390
  9.9 5.9 %collective-permute-start.5 = (f32[2,64,128]{2,1,0:T(8,128)S(1)}, f32[2,64,128]{2,1,0:T(8,128)S(1)}, u32[]{:S(2)}, u32[]{:S(2)}) collective-permute-start(f32[2,64,128]{2,1,0:T(8,128)S(1)} %folded.7.a_ref), channel_id=1, source_target_pairs={{0,2},{1,3},{2,0},{3,1},{4,6},{5,7},{6,4},{7,5},{8,10},{9,11},{10,... | collective-permute-start | bytes 196616 | tf_op jit(solution)/shard_map/ppermute | solution.py:397
  12.7 27.6 %collective-permute-start.11 = (bf16[1024,128]{1,0:T(8,128)(2,1)S(1)}, bf16[1024,128]{1,0:T(8,128)(2,1)S(1)}, u32[]{:S(2)}, u32[]{:S(2)}) collective-permute-start(bf16[1024,128]{1,0:T(8,128)(2,1)S(1)} %collective-permute-done.2.after_ref.refs_4_), channel_id=1, source_target_pairs={{0,16},{16,0},{32,48},{48,32},{64,80},{80,64},{96,112},{112,96},{1... | collective-permute-start | bytes 786440 | tf_op jit(solution)/shard_map/ppermute | solution.py:405
  12.7 8.4 %collective-permute-start.4 = (bf16[1024,128]{1,0:T(8,128)(2,1)S(1)}, bf16[1024,128]{1,0:T(8,128)(2,1)S(1)}, u32[]{:S(2)}, u32[]{:S(2)}) collective-permute-start(bf16[1024,128]{1,0:T(8,128)(2,1)S(1)} %collective-permute-done.2.after_ref.refs_4_), channel_id=1, source_target_pairs={{0,32},{32,64},{64,96},{96,128},{128,160},{160,192},{192,224},{224... | collective-permute-start | bytes 786440 | tf_op jit(solution)/shard_map/ppermute | solution.py:392
  15.8 5.3 %collective-permute-start.6 = (f32[2,64,128]{2,1,0:T(8,128)S(1)}, f32[2,64,128]{2,1,0:T(8,128)S(1)}, u32[]{:S(2)}, u32[]{:S(2)}) collective-permute-start(f32[2,64,128]{2,1,0:T(8,128)S(1)} %folded.8.a_ref), channel_id=1, source_target_pairs={{0,4},{1,5},{2,6},{3,7},{4,0},{5,1},{6,2},{7,3},{8,12},{9,13},{10,... | collective-permute-start | bytes 196616 | tf_op jit(solution)/shard_map/ppermute | solution.py:400
  21.2 19.2 %collective-permute-start.12 = (bf16[1024,128]{1,0:T(8,128)(2,1)S(1)}, bf16[1024,128]{1,0:T(8,128)(2,1)S(1)}, u32[]{:S(2)}, u32[]{:S(2)}) collective-permute-start(bf16[1024,128]{1,0:T(8,128)(2,1)S(1)} %collective-permute-done.4.after_ref.refs_5_), channel_id=1, source_target_pairs={{0,16},{16,0},{32,48},{48,32},{64,80},{80,64},{96,112},{112,96},{1... | collective-permute-start | bytes 786440 | tf_op jit(solution)/shard_map/ppermute | solution.py:405
  21.4 8.8 %collective-permute-start.7 = (bf16[1024,128]{1,0:T(8,128)(2,1)S(1)}, bf16[1024,128]{1,0:T(8,128)(2,1)S(1)}, u32[]{:S(2)}, u32[]{:S(2)}) collective-permute-start(bf16[1024,128]{1,0:T(8,128)(2,1)S(1)} %collective-permute-done.4.after_ref.refs_5_), channel_id=1, source_target_pairs={{0,32},{32,64},{64,96},{96,128},{128,160},{160,192},{192,224},{224... | collective-permute-start | bytes 786440 | tf_op jit(solution)/shard_map/ppermute | solution.py:392
  23.4 6.8 %collective-permute-start.8 = (f32[2,64,128]{2,1,0:T(8,128)S(1)}, f32[2,64,128]{2,1,0:T(8,128)S(1)}, u32[]{:S(2)}, u32[]{:S(2)}) collective-permute-start(f32[2,64,128]{2,1,0:T(8,128)S(1)} %folded.9.a_ref), channel_id=1, source_target_pairs={{0,8},{1,9},{2,10},{3,11},{4,12},{5,13},{6,14},{7,15},{8,0},{9,1},... | collective-permute-start | bytes 196616 | tf_op jit(solution)/shard_map/ppermute | solution.py:400
  30.2 10.9 %collective-permute-start.13 = (bf16[1024,128]{1,0:T(8,128)(2,1)S(1)}, bf16[1024,128]{1,0:T(8,128)(2,1)S(1)}, u32[]{:S(2)}, u32[]{:S(2)}) collective-permute-start(bf16[1024,128]{1,0:T(8,128)(2,1)S(1)} %collective-permute-done.7.after_ref.refs_6_), channel_id=1, source_target_pairs={{0,16},{16,0},{32,48},{48,32},{64,80},{80,64},{96,112},{112,96},{1... | collective-permute-start | bytes 786440 | tf_op jit(solution)/shard_map/ppermute | solution.py:405
  31.5 9.6 %copy-start = (s32[512]{0:T(512)S(1)}, s32[512]{0:T(512)}, u32[]{:S(2)}) copy-start(s32[512]{0:T(512)} %refs_0_.1) | copy-start | bytes 6148
  31.5 9.6 %copy-start.1 = (s32[512]{0:T(512)S(1)}, s32[512]{0:T(512)}, u32[]{:S(2)}) copy-start(s32[512]{0:T(512)} %refs_1_.1) | copy-start | bytes 6148
  31.5 7.9 %collective-permute-start.10 = (f32[2,64,128]{2,1,0:T(8,128)S(1)}, f32[2,64,128]{2,1,0:T(8,128)S(1)}, u32[]{:S(2)}, u32[]{:S(2)}) collective-permute-start(f32[2,64,128]{2,1,0:T(8,128)S(1)} %folded.10.a_ref), channel_id=1, source_target_pairs={{0,32},{16,48},{32,0},{48,16},{64,96},{80,112},{96,64},{112,80},{1... | collective-permute-start | bytes 196616 | tf_op jit(solution)/shard_map/ppermute | solution.py:400
  33.2 6.2 %collective-permute-start.9 = (bf16[512,128]{1,0:T(8,128)(2,1)S(1)}, bf16[512,128]{1,0:T(8,128)(2,1)S(1)}, u32[]{:S(2)}, u32[]{:S(2)}) collective-permute-start(bf16[512,128]{1,0:T(8,128)(2,1)S(1)} %slice.3), channel_id=1, source_target_pairs={{0,32},{32,64},{64,96},{96,128},{128,160},{160,192},{192,224},{224... | collective-permute-start | bytes 393224 | tf_op jit(solution)/shard_map/ppermute | solution.py:392
  39.4 1.6 %collective-permute-start.14 = (bf16[512,128]{1,0:T(8,128)(2,1)S(1)}, bf16[512,128]{1,0:T(8,128)(2,1)S(1)}, u32[]{:S(2)}, u32[]{:S(2)}) collective-permute-start(bf16[512,128]{1,0:T(8,128)(2,1)S(1)} %collective-permute-done.9.refs_7_), channel_id=1, source_target_pairs={{0,16},{16,0},{32,48},{48,32},{64,80},{80,64},{96,112},{112,96},{1... | collective-permute-start | bytes 393224 | tf_op jit(solution)/shard_map/ppermute | solution.py:405
  44.7 14.8 %collective-permute-start.16 = (s16[1040,128]{1,0:T(8,128)(2,1)S(1)}, s16[1040,128]{1,0:T(8,128)(2,1)S(1)}, u32[]{:S(2)}, u32[]{:S(2)}) collective-permute-start(s16[1040,128]{1,0:T(8,128)(2,1)S(1)} %get-tuple-element.68), channel_id=1, source_target_pairs={{0,1},{1,2},{2,3},{3,0},{4,5},{5,6},{6,7},{7,4},{8,9},{9,10},{10,1... | collective-permute-start | bytes 798728 | tf_op jit(solution)/shard_map/ppermute | solution.py:378
  46.3 14.8 %collective-permute-start.17 = (s16[1040,128]{1,0:T(8,128)(2,1)S(1)}, s16[1040,128]{1,0:T(8,128)(2,1)S(1)}, u32[]{:S(2)}, u32[]{:S(2)}) collective-permute-start(s16[1040,128]{1,0:T(8,128)(2,1)S(1)} %get-tuple-element.69), channel_id=1, source_target_pairs={{0,2},{1,3},{2,0},{3,1},{4,6},{5,7},{6,4},{7,5},{8,10},{9,11},{10,... | collective-permute-start | bytes 798728 | tf_op jit(solution)/shard_map/ppermute | solution.py:378
  49.0 12.1 %collective-permute-start.18 = (s16[1040,128]{1,0:T(8,128)(2,1)S(1)}, s16[1040,128]{1,0:T(8,128)(2,1)S(1)}, u32[]{:S(2)}, u32[]{:S(2)}) collective-permute-start(s16[1040,128]{1,0:T(8,128)(2,1)S(1)} %get-tuple-element.70), channel_id=1, source_target_pairs={{0,3},{1,0},{2,1},{3,2},{4,7},{5,4},{6,5},{7,6},{8,11},{9,8},{10,9... | collective-permute-start | bytes 798728 | tf_op jit(solution)/shard_map/ppermute | solution.py:378
  52.3 5.3 %collective-permute-start.15 = (f32[2,64,128]{2,1,0:T(8,128)S(1)}, f32[2,64,128]{2,1,0:T(8,128)S(1)}, u32[]{:S(2)}, u32[]{:S(2)}) collective-permute-start(f32[2,64,128]{2,1,0:T(8,128)S(1)} %folded.11.a_ref), channel_id=1, source_target_pairs={{0,64},{16,80},{32,96},{48,112},{64,0},{80,16},{96,32},{112,48},{1... | collective-permute-start | bytes 196616 | tf_op jit(solution)/shard_map/ppermute | solution.py:412
  53.7 14.2 %collective-permute-start.22 = (s16[1040,128]{1,0:T(8,128)(2,1)S(1)}, s16[1040,128]{1,0:T(8,128)(2,1)S(1)}, u32[]{:S(2)}, u32[]{:S(2)}) collective-permute-start(s16[1040,128]{1,0:T(8,128)(2,1)S(1)} %get-tuple-element.75), channel_id=1, source_target_pairs={{0,4},{1,5},{2,6},{3,7},{4,8},{5,9},{6,10},{7,11},{8,12},{9,13},{1... | collective-permute-start | bytes 798728 | tf_op jit(solution)/shard_map/ppermute | solution.py:378
  57.6 10.4 %collective-permute-start.23 = (s16[1040,128]{1,0:T(8,128)(2,1)S(1)}, s16[1040,128]{1,0:T(8,128)(2,1)S(1)}, u32[]{:S(2)}, u32[]{:S(2)}) collective-permute-start(s16[1040,128]{1,0:T(8,128)(2,1)S(1)} %get-tuple-element.76), channel_id=1, source_target_pairs={{0,8},{1,9},{2,10},{3,11},{4,12},{5,13},{6,14},{7,15},{8,0},{9,1},... | collective-permute-start | bytes 798728 | tf_op jit(solution)/shard_map/ppermute | solution.py:378
  59.5 10.4 %collective-permute-start.24 = (s16[1040,128]{1,0:T(8,128)(2,1)S(1)}, s16[1040,128]{1,0:T(8,128)(2,1)S(1)}, u32[]{:S(2)}, u32[]{:S(2)}) collective-permute-start(s16[1040,128]{1,0:T(8,128)(2,1)S(1)} %get-tuple-element.77), channel_id=1, source_target_pairs={{0,12},{1,13},{2,14},{3,15},{4,0},{5,1},{6,2},{7,3},{8,4},{9,5},{1... | collective-permute-start | bytes 798728 | tf_op jit(solution)/shard_map/ppermute | solution.py:378
  61.7 9.6 %collective-permute-start.28 = (f32[2,64,128]{2,1,0:T(8,128)S(1)}, f32[2,64,128]{2,1,0:T(8,128)S(1)}, u32[]{:S(2)}, u32[]{:S(2)}) collective-permute-start(f32[2,64,128]{2,1,0:T(8,128)S(1)} %folded.12.a_ref), channel_id=1, source_target_pairs={{0,128},{16,144},{32,160},{48,176},{64,192},{80,208},{96,224},{112... | collective-permute-start | bytes 196616 | tf_op jit(solution)/shard_map/ppermute | solution.py:417
  70.5 5.6 %collective-permute-start.25 = (s16[272,128]{1,0:T(8,128)(2,1)S(1)}, s16[272,128]{1,0:T(8,128)(2,1)S(1)}, u32[]{:S(2)}, u32[]{:S(2)}) collective-permute-start(s16[272,128]{1,0:T(8,128)(2,1)S(1)} %get-tuple-element.79), channel_id=1, source_target_pairs={{0,1},{1,2},{2,3},{3,0},{4,5},{5,6},{6,7},{7,4},{8,9},{9,10},{10,1... | collective-permute-start | bytes 208904 | tf_op jit(solution)/shard_map/ppermute | solution.py:378
  71.3 7.0 %collective-permute-start.29 = (f32[64,128]{1,0:T(8,128)S(1)}, f32[64,128]{1,0:T(8,128)S(1)}, u32[]{:S(2)}, u32[]{:S(2)}) collective-permute-start(f32[64,128]{1,0:T(8,128)S(1)} %folded.13.mine_ref), channel_id=1, source_target_pairs={{0,16},{16,0},{32,48},{48,32},{64,80},{80,64},{96,112},{112,96},{1... | collective-permute-start | bytes 98312 | tf_op jit(solution)/shard_map/ppermute | solution.py:421
  71.4 13.2 %collective-permute-start.26 = (s16[272,128]{1,0:T(8,128)(2,1)S(1)}, s16[272,128]{1,0:T(8,128)(2,1)S(1)}, u32[]{:S(2)}, u32[]{:S(2)}) collective-permute-start(s16[272,128]{1,0:T(8,128)(2,1)S(1)} %get-tuple-element.80), channel_id=1, source_target_pairs={{0,2},{1,3},{2,0},{3,1},{4,6},{5,7},{6,4},{7,5},{8,10},{9,11},{10,... | collective-permute-start | bytes 208904 | tf_op jit(solution)/shard_map/ppermute | solution.py:378
  72.9 11.8 %collective-permute-start.27 = (s16[272,128]{1,0:T(8,128)(2,1)S(1)}, s16[272,128]{1,0:T(8,128)(2,1)S(1)}, u32[]{:S(2)}, u32[]{:S(2)}) collective-permute-start(s16[272,128]{1,0:T(8,128)(2,1)S(1)} %get-tuple-element.81), channel_id=1, source_target_pairs={{0,3},{1,0},{2,1},{3,2},{4,7},{5,4},{6,5},{7,6},{8,11},{9,8},{10,9... | collective-permute-start | bytes 208904 | tf_op jit(solution)/shard_map/ppermute | solution.py:378
  74.3 10.3 %collective-permute-start.19 = (s16[272,128]{1,0:T(8,128)(2,1)S(1)}, s16[272,128]{1,0:T(8,128)(2,1)S(1)}, u32[]{:S(2)}, u32[]{:S(2)}) collective-permute-start(s16[272,128]{1,0:T(8,128)(2,1)S(1)} %get-tuple-element.72), channel_id=1, source_target_pairs={{0,4},{1,5},{2,6},{3,7},{4,8},{5,9},{6,10},{7,11},{8,12},{9,13},{1... | collective-permute-start | bytes 208904 | tf_op jit(solution)/shard_map/ppermute | solution.py:378
  76.1 8.6 %collective-permute-start.20 = (s16[272,128]{1,0:T(8,128)(2,1)S(1)}, s16[272,128]{1,0:T(8,128)(2,1)S(1)}, u32[]{:S(2)}, u32[]{:S(2)}) collective-permute-start(s16[272,128]{1,0:T(8,128)(2,1)S(1)} %get-tuple-element.73), channel_id=1, source_target_pairs={{0,8},{1,9},{2,10},{3,11},{4,12},{5,13},{6,14},{7,15},{8,0},{9,1},... | collective-permute-start | bytes 208904 | tf_op jit(solution)/shard_map/ppermute | solution.py:378
  78.4 6.3 %collective-permute-start.21 = (s16[272,128]{1,0:T(8,128)(2,1)S(1)}, s16[272,128]{1,0:T(8,128)(2,1)S(1)}, u32[]{:S(2)}, u32[]{:S(2)}) collective-permute-start(s16[272,128]{1,0:T(8,128)(2,1)S(1)} %get-tuple-element.74), channel_id=1, source_target_pairs={{0,12},{1,13},{2,14},{3,15},{4,0},{5,1},{6,2},{7,3},{8,4},{9,5},{1... | collective-permute-start | bytes 208904 | tf_op jit(solution)/shard_map/ppermute | solution.py:378
  (2 other events, 12.1 us)
where the time goes:
time: 86.5 us; the launch traced here: 85.9 us
  starting transfers between devices  42.9 us (50%)
  Pallas kernels  27.6 us (32%)
  waiting for transfers between devices  12.7 us (15%)
  local copies, waits for them, and re-layouts  1.75 us (2%)
  between operations  0.97 us (1%)
    ppermute x12, starting transfers between devices, along(): lax.ppermute(xs[k - 1], 'cols', moved(k))  18.2 us
    pallas_call x4, Pallas kernels, build_weights(): pl.pallas_call(functools.partial(build_body, block=block), grid=(1,), in_...  15.1 us
    ppermute x4, starting transfers between devices, on_device(): lax.ppermute(found[-1] if step < 3 else found[-1][:2 * ROWS], 'rows', aro...  8.24 us
    ppermute x12, waiting for transfers between devices, along(): lax.ppermute(xs[k - 1], 'cols', moved(k))  7.12 us
    ppermute x3, starting transfers between devices, on_device(): lax.ppermute(grams, *(('cols', swapped(2 << step)) if step < 3 else ('row...  6.38 us
    pallas_call x2, Pallas kernels, products(): pl.pallas_call(functools.partial(product_body, along_x=along_x, sizes=siz...  5.49 us
    pallas_call x1, Pallas kernels, inverted(): pl.pallas_call(functools.partial(inverse_body, me=me), in_specs=[in_vmem,...  4.27 us
    ppermute x1, waiting for transfers between devices, on_device(): more = lax.ppermute(grams, 'rows', swapped(4))  3.73 us
  transfers between devices with their start and end apart: 30, of which 7 were waited for; matrix products, arithmetic and copies ran while one was open for 2% of the time, Pallas kernels for 26%

commit v1 on v0

--- a/solution.py
+++ b/solution.py
@@ -200,7 +200,7 @@
         out_shape=out_shape,
         scratch_shapes=scratch,
         compiler_params=pltpu.CompilerParams(vmem_limit_bytes=24 * MIB),
-        cost_estimate=pl.CostEstimate(flops=4 * 10**9, bytes_accessed=13 * 10**6, transcendentals=0),
+        cost_estimate=pl.CostEstimate(flops=2 * 10**9, bytes_accessed=6 * 10**6, transcendentals=0),
         name="products",
         interpret=interpret,
     )(*operands, *highs, *lows)
@@ -234,7 +234,7 @@
         + [jax.ShapeDtypeStruct((RANK, OWN // 2), jnp.float32)],
         scratch_shapes=[pltpu.VMEM((SIDE, RANK, OWN // 2), jnp.float32)],
         compiler_params=pltpu.CompilerParams(vmem_limit_bytes=20 * MIB),
-        cost_estimate=pl.CostEstimate(flops=2 * 10**9, bytes_accessed=7 * 10**6, transcendentals=0),
+        cost_estimate=pl.CostEstimate(flops=10**8, bytes_accessed=10**6, transcendentals=0),
         name="relayed",
         interpret=interpret,
     )(own, *received)
@@ -386,23 +386,19 @@
     others = [lax.ppermute(x, "rows", across) for x in (factor_items, factor_words)]
     found = [jnp.concatenate([factor_items, factor_words, *others], axis=0)]
     highs, lows = [], []
-    grams = partial_grams(found)
-    more = lax.ppermute(grams, "cols", swapped(1))
     for step in range(4):
         arriving = lax.ppermute(found[-1] if step < 3 else found[-1][: 2 * ROWS], "rows", around)
+        grams = folded(found[-1], grams, more) if step else partial_grams(found)
+        more = lax.ppermute(grams, "cols", swapped(1 << step))
         high, low = build_weights(values, tile_users, step, found[-1])
-        if step == 0:
-            grams = folded(found[-1], grams, more)
-            arriving, low, grams = after((arriving, low, grams))
-            more = lax.ppermute(grams, "cols", swapped(2))
-        else:
-            grams = folded(found[-1], grams, more)
-            more = lax.ppermute(grams, *(("cols", swapped(2 << step)) if step < 3 else ("rows", swapped(2))))
-            arriving, low, more = after((arriving, low, more))
+        arriving, low, more = after((arriving, low, more))
         highs.append(high)
         lows.append(low)
         found.append(arriving)
+    grams = folded(low, grams, more)
+    more = lax.ppermute(grams, "rows", swapped(2))
     pieces = found + [lax.ppermute(x, "rows", across) for x in found[1:]]
+    *pieces, more = after((*pieces, more))
     scalars = (tile_items, tile_words, tile_count)
     *out, own_a, parts = products(True, highs, lows, pieces=pieces, scalars=scalars)
     in_a = along(out, True)
@@ -410,11 +406,13 @@
     in_b = along(out, False)
     grams = folded(own_b, grams, more)
     more = lax.ppermute(grams, "rows", swapped(4))
-    own_a, more = after((own_a, more))
+    *in_a, more = after((*in_a, more))
     *out, own_a = relayed(True, own_a, in_a)
     end_a = along(out, False)
     grams = folded(own_a, grams, more)
     more = lax.ppermute(grams, "rows", swapped(8))
+    tied = after((*in_b, *end_a))
+    in_b, end_a = tied[: SIDE - 1], tied[SIDE - 1 :]
     *out, own_b = relayed(False, own_b, in_b)
     end_b = along(out, True)
     grams = folded(own_b, grams, more, multiply=True)

time: 86.5 us -> 90.5 us (1.046)
  waiting for transfers between devices: 12.7 us -> 16.7 us
    ppermute x1, waiting for transfers between devices: 0.01 us -> 3.9 us  [on_device(): more = lax.ppermute(grams, 'rows', swapped(8))]
    ppermute x1, waiting for transfers between devices: 3.73 us -> 0.01 us  [on_device(): more = lax.ppermute(grams, 'rows', swapped(4))]
    ppermute x12, waiting for transfers between devices: 7.12 us -> 10.7 us  [along(): lax.ppermute(xs[k - 1], 'cols', moved(k))]
    ppermute x12, starting transfers between devices: 18.2 us -> 15.7 us  [along(): lax.ppermute(xs[k - 1], 'cols', moved(k))]
    ppermute x1, starting transfers between devices: 1.39 us -> 2.73 us  [on_device(): more = lax.ppermute(grams, 'rows', swapped(4))]
    ppermute x5, waiting for transfers between devices: 1.13 us -> 2.1 us  [the longest x1 2.09 us: on_device(): more = lax.ppermute(grams, 'rows', swapped(2))]
  transfers between devices with their start and end apart: 30 -> 30, of which waited for: 7 -> 7; matrix products, arithmetic and copies ran while one was open for 2% -> 2% of each run, Pallas kernels for 26% -> 25%
where the time goes in v1:
time: 90.5 us; the launch traced here: 89.4 us
  starting transfers between devices  42.4 us (47%)
  Pallas kernels  27.5 us (30%)
  waiting for transfers between devices  16.7 us (18%)
  local copies, waits for them, and re-layouts  1.75 us (2%)
  between operations  0.99 us (1%)
    ppermute x12, starting transfers between devices, along(): lax.ppermute(xs[k - 1], 'cols', moved(k))  15.7 us
    pallas_call x4, Pallas kernels, build_weights(): pl.pallas_call(functools.partial(build_body, block=block), grid=(1,), in_...  15 us
    ppermute x12, waiting for transfers between devices, along(): lax.ppermute(xs[k - 1], 'cols', moved(k))  10.7 us
    ppermute x4, starting transfers between devices, on_device(): more = lax.ppermute(grams, 'cols', swapped(1 << step))  8.96 us
    ppermute x4, starting transfers between devices, on_device(): lax.ppermute(found[-1] if step < 3 else found[-1][:2 * ROWS], 'rows', aro...  8.37 us
    pallas_call x2, Pallas kernels, products(): pl.pallas_call(functools.partial(product_body, along_x=along_x, sizes=siz...  5.5 us
    pallas_call x1, Pallas kernels, inverted(): pl.pallas_call(functools.partial(inverse_body, me=me), in_specs=[in_vmem,...  4.27 us
    ppermute x1, waiting for transfers between devices, on_device(): more = lax.ppermute(grams, 'rows', swapped(8))  3.9 us
  transfers between devices with their start and end apart: 30, of which 7 were waited for; matrix products, arithmetic and copies ran while one was open for 2% of the time, Pallas kernels for 25%

profile of v1, /device:TPU:32, one launch (start us, length us, event | category | flops | bytes accessed | tf_op | source)
XLA Modules:
  0.0 89.4 jit_solution(5688762603926913991)
XLA Ops:
  2.6 2.0 %collective-permute-start.2 = (bf16[1024,128]{1,0:T(8,128)(2,1)S(1)}, bf16[1024,128]{1,0:T(8,128)(2,1)S(1)}, u32[]{:S(2)}, u32[]{:S(2)}) collective-permute-start(bf16[1024,128]{1,0:T(8,128)(2,1)S(1)} %constant_dynamic-update-slice_fusion.after_ref.refs_0_.refs_3_), channel_id=1, source_target_pairs={{0,32},{32,64},{64,96},{96,128},{128,160},{160,192},{192,224},{224... | collective-permute-start | bytes 786440 | tf_op jit(solution)/shard_map/ppermute | solution.py:390
  4.5 1.5 %collective-permute-start.3 = (f32[2,64,128]{2,1,0:T(8,128)S(1)}, f32[2,64,128]{2,1,0:T(8,128)S(1)}, u32[]{:S(2)}, u32[]{:S(2)}) collective-permute-start(f32[2,64,128]{2,1,0:T(8,128)S(1)} %partial_grams.1.a_ref), channel_id=1, source_target_pairs={{0,1},{1,0},{2,3},{3,2},{4,5},{5,4},{6,7},{7,6},{8,9},{9,8},{10,11... | collective-permute-start | bytes 196616 | tf_op jit(solution)/shard_map/ppermute | solution.py:392
  6.0 3.8 %build_weights.4 = (bf16[64,128,128]{2,1,0:T(8,128)(2,1)S(1)}, bf16[64,128,128]{2,1,0:T(8,128)(2,1)S(1)}) custom-call(f32[512,128]{1,0:T(8,128)S(1)} %copy-done.2, s32[512,128]{1,0:T(8,128)S(1)} %copy-done.3, bf16[1024,128]{1,0:T(8,128)(2,1)S(1)} %constant_dynamic-update-slice_fusion.after_ref.refs_0_.refs_3_), custom_call_target="tpu_custom_call" | custom-call | flops 6000000000 | bytes 20000000 | tf_op jit(solution)/shard_map/build_weights/pallas_call | solution.py:71
  10.0 2.0 %collective-permute-start.4 = (bf16[1024,128]{1,0:T(8,128)(2,1)S(1)}, bf16[1024,128]{1,0:T(8,128)(2,1)S(1)}, u32[]{:S(2)}, u32[]{:S(2)}) collective-permute-start(bf16[1024,128]{1,0:T(8,128)(2,1)S(1)} %collective-permute-done.2.after_ref.refs_4_), channel_id=1, source_target_pairs={{0,32},{32,64},{64,96},{96,128},{128,160},{160,192},{192,224},{224... | collective-permute-start | bytes 786440 | tf_op jit(solution)/shard_map/ppermute | solution.py:390
  12.0 2.8 %collective-permute-start.5 = (f32[2,64,128]{2,1,0:T(8,128)S(1)}, f32[2,64,128]{2,1,0:T(8,128)S(1)}, u32[]{:S(2)}, u32[]{:S(2)}) collective-permute-start(f32[2,64,128]{2,1,0:T(8,128)S(1)} %folded.7.a_ref), channel_id=1, source_target_pairs={{0,2},{1,3},{2,0},{3,1},{4,6},{5,7},{6,4},{7,5},{8,10},{9,11},{10,... | collective-permute-start | bytes 196616 | tf_op jit(solution)/shard_map/ppermute | solution.py:392
  14.8 3.7 %build_weights.5 = (bf16[64,128,128]{2,1,0:T(8,128)(2,1)S(1)}, bf16[64,128,128]{2,1,0:T(8,128)(2,1)S(1)}) custom-call(f32[512,128]{1,0:T(8,128)S(1)} %copy-done.2, s32[512,128]{1,0:T(8,128)S(1)} %copy-done.3, bf16[1024,128]{1,0:T(8,128)(2,1)S(1)} %collective-permute-done.2.after_ref.refs_4_), custom_call_target="tpu_custom_call" | custom-call | flops 6000000000 | bytes 20000000 | tf_op jit(solution)/shard_map/build_weights/pallas_call | solution.py:71
  18.5 1.3 %collective-permute-start.11 = (bf16[1024,128]{1,0:T(8,128)(2,1)S(1)}, bf16[1024,128]{1,0:T(8,128)(2,1)S(1)}, u32[]{:S(2)}, u32[]{:S(2)}) collective-permute-start(bf16[1024,128]{1,0:T(8,128)(2,1)S(1)} %collective-permute-done.4.after_ref.refs_5_), channel_id=1, source_target_pairs={{0,16},{16,0},{32,48},{48,32},{64,80},{80,64},{96,112},{112,96},{1... | collective-permute-start | bytes 786440 | tf_op jit(solution)/shard_map/ppermute | solution.py:400
  19.8 2.0 %collective-permute-start.6 = (bf16[1024,128]{1,0:T(8,128)(2,1)S(1)}, bf16[1024,128]{1,0:T(8,128)(2,1)S(1)}, u32[]{:S(2)}, u32[]{:S(2)}) collective-permute-start(bf16[1024,128]{1,0:T(8,128)(2,1)S(1)} %collective-permute-done.4.after_ref.refs_5_), channel_id=1, source_target_pairs={{0,32},{32,64},{64,96},{96,128},{128,160},{160,192},{192,224},{224... | collective-permute-start | bytes 786440 | tf_op jit(solution)/shard_map/ppermute | solution.py:390
  21.8 1.7 %collective-permute-start.7 = (f32[2,64,128]{2,1,0:T(8,128)S(1)}, f32[2,64,128]{2,1,0:T(8,128)S(1)}, u32[]{:S(2)}, u32[]{:S(2)}) collective-permute-start(f32[2,64,128]{2,1,0:T(8,128)S(1)} %folded.8.a_ref), channel_id=1, source_target_pairs={{0,4},{1,5},{2,6},{3,7},{4,0},{5,1},{6,2},{7,3},{8,12},{9,13},{10,... | collective-permute-start | bytes 196616 | tf_op jit(solution)/shard_map/ppermute | solution.py:392
  23.5 3.8 %build_weights.6 = (bf16[64,128,128]{2,1,0:T(8,128)(2,1)S(1)}, bf16[64,128,128]{2,1,0:T(8,128)(2,1)S(1)}) custom-call(f32[512,128]{1,0:T(8,128)S(1)} %copy-done.2, s32[512,128]{1,0:T(8,128)S(1)} %copy-done.3, bf16[1024,128]{1,0:T(8,128)(2,1)S(1)} %collective-permute-done.4.after_ref.refs_5_), custom_call_target="tpu_custom_call" | custom-call | flops 6000000000 | bytes 20000000 | tf_op jit(solution)/shard_map/build_weights/pallas_call | solution.py:71
  27.5 3.0 %collective-permute-start.9 = (f32[2,64,128]{2,1,0:T(8,128)S(1)}, f32[2,64,128]{2,1,0:T(8,128)S(1)}, u32[]{:S(2)}, u32[]{:S(2)}) collective-permute-start(f32[2,64,128]{2,1,0:T(8,128)S(1)} %folded.9.a_ref), channel_id=1, source_target_pairs={{0,8},{1,9},{2,10},{3,11},{4,12},{5,13},{6,14},{7,15},{8,0},{9,1},... | collective-permute-start | bytes 196616 | tf_op jit(solution)/shard_map/ppermute | solution.py:392
  30.5 2.4 %collective-permute-start.8 = (bf16[512,128]{1,0:T(8,128)(2,1)S(1)}, bf16[512,128]{1,0:T(8,128)(2,1)S(1)}, u32[]{:S(2)}, u32[]{:S(2)}) collective-permute-start(bf16[512,128]{1,0:T(8,128)(2,1)S(1)} %slice.3), channel_id=1, source_target_pairs={{0,32},{32,64},{64,96},{96,128},{128,160},{160,192},{192,224},{224... | collective-permute-start | bytes 393224 | tf_op jit(solution)/shard_map/ppermute | solution.py:390
  32.8 3.7 %build_weights.7 = (bf16[64,128,128]{2,1,0:T(8,128)(2,1)S(1)}, bf16[64,128,128]{2,1,0:T(8,128)(2,1)S(1)}) custom-call(f32[512,128]{1,0:T(8,128)S(1)} %copy-done.2, s32[512,128]{1,0:T(8,128)S(1)} %copy-done.3, bf16[1024,128]{1,0:T(8,128)(2,1)S(1)} %collective-permute-done.6.after_ref.refs_6_), custom_call_target="tpu_custom_call" | custom-call | flops 6000000000 | bytes 20000000 | tf_op jit(solution)/shard_map/build_weights/pallas_call | solution.py:71
  36.7 2.6 %collective-permute-start.14 = (f32[2,64,128]{2,1,0:T(8,128)S(1)}, f32[2,64,128]{2,1,0:T(8,128)S(1)}, u32[]{:S(2)}, u32[]{:S(2)}) collective-permute-start(f32[2,64,128]{2,1,0:T(8,128)S(1)} %folded.10.a_ref), channel_id=1, source_target_pairs={{0,32},{16,48},{32,0},{48,16},{64,96},{80,112},{96,64},{112,80},{1... | collective-permute-start | bytes 196616 | tf_op jit(solution)/shard_map/ppermute | solution.py:399
  40.0 2.1 %collective-permute-done.14.b_ref = f32[2,64,128]{2,1,0:T(8,128)S(1)} collective-permute-done((f32[2,64,128]{2,1,0:T(8,128)S(1)}, f32[2,64,128]{2,1,0:T(8,128)S(1)}, u32[]{:S(2)}, u32[]{:S(2)}) %collective-permute-start.14) | collective-permute-done | bytes 65568 | tf_op jit(solution)/shard_map/ppermute | solution.py:399
  42.1 3.7 %products.2 = (s16[1040,128]{1,0:T(8,128)(2,1)S(1)}, s16[1040,128]{1,0:T(8,128)(2,1)S(1)}, s16[1040,128]{1,0:T(8,128)(2,1)S(1)}, f32[4,128,256]{2,1,0:T(8,128)S(1)}, bf16[256,512]{1,0:T(8,128)(2,1)S(1)}) custom-call(s32[512]{0:T(512)S(1)} %copy-done, s32[512]{0:T(512)S(1)} %copy-done.1, s32[1]{0:T(128)S(6)} %copy.11.refs_2_, ...), custom_call_target="tpu_custom_call" | custom-call | flops 2000000000 | bytes 6000000 | tf_op jit(solution)/shard_map/products/pallas_call | solution.py:196
  46.4 1.8 %products.3 = (s16[1040,128]{1,0:T(8,128)(2,1)S(1)}, s16[1040,128]{1,0:T(8,128)(2,1)S(1)}, s16[1040,128]{1,0:T(8,128)(2,1)S(1)}, f32[4,128,256]{2,1,0:T(8,128)S(1)}) custom-call(bf16[256,512]{1,0:T(8,128)(2,1)S(1)} %get-tuple-element.95.refs_0_, bf16[64,128,128]{2,1,0:T(8,128)(2,1)S(1)} %get-tuple-element.84.refs_12_.refs_1_, ...), custom_call_target="tpu_custom_call" | custom-call | flops 2000000000 | bytes 6000000 | tf_op jit(solution)/shard_map/products/pallas_call | solution.py:196
  48.3 2.7 %collective-permute-start.18 = (f32[2,64,128]{2,1,0:T(8,128)S(1)}, f32[2,64,128]{2,1,0:T(8,128)S(1)}, u32[]{:S(2)}, u32[]{:S(2)}) collective-permute-start(f32[2,64,128]{2,1,0:T(8,128)S(1)} %folded.11.a_ref), channel_id=1, source_target_pairs={{0,64},{16,80},{32,96},{48,112},{64,0},{80,16},{96,32},{112,48},{1... | collective-permute-start | bytes 196616 | tf_op jit(solution)/shard_map/ppermute | solution.py:408
  51.0 2.7 %collective-permute-start.16 = (s16[1040,128]{1,0:T(8,128)(2,1)S(1)}, s16[1040,128]{1,0:T(8,128)(2,1)S(1)}, u32[]{:S(2)}, u32[]{:S(2)}) collective-permute-start(s16[1040,128]{1,0:T(8,128)(2,1)S(1)} %get-tuple-element.93), channel_id=1, source_target_pairs={{0,2},{1,3},{2,0},{3,1},{4,6},{5,7},{6,4},{7,5},{8,10},{9,11},{10,... | collective-permute-start | bytes 798728 | tf_op jit(solution)/shard_map/ppermute | solution.py:378
  53.8 1.4 %collective-permute-start.17 = (s16[1040,128]{1,0:T(8,128)(2,1)S(1)}, s16[1040,128]{1,0:T(8,128)(2,1)S(1)}, u32[]{:S(2)}, u32[]{:S(2)}) collective-permute-start(s16[1040,128]{1,0:T(8,128)(2,1)S(1)} %get-tuple-element.94), channel_id=1, source_target_pairs={{0,3},{1,0},{2,1},{3,2},{4,7},{5,4},{6,5},{7,6},{8,11},{9,8},{10,9... | collective-permute-start | bytes 798728 | tf_op jit(solution)/shard_map/ppermute | solution.py:378
  55.9 1.8 %collective-permute-start.20 = (s16[1040,128]{1,0:T(8,128)(2,1)S(1)}, s16[1040,128]{1,0:T(8,128)(2,1)S(1)}, u32[]{:S(2)}, u32[]{:S(2)}) collective-permute-start(s16[1040,128]{1,0:T(8,128)(2,1)S(1)} %get-tuple-element.103), channel_id=1, source_target_pairs={{0,8},{1,9},{2,10},{3,11},{4,12},{5,13},{6,14},{7,15},{8,0},{9,1},... | collective-permute-start | bytes 798728 | tf_op jit(solution)/shard_map/ppermute | solution.py:378
  57.7 3.2 %collective-permute-done.15.a_ref = s16[1040,128]{1,0:T(8,128)(2,1)S(1)} collective-permute-done((s16[1040,128]{1,0:T(8,128)(2,1)S(1)}, s16[1040,128]{1,0:T(8,128)(2,1)S(1)}, u32[]{:S(2)}, u32[]{:S(2)}) %collective-permute-start.15) | collective-permute-done | bytes 266272 | tf_op jit(solution)/shard_map/ppermute | solution.py:378
  62.0 2.9 %collective-permute-done.17.c_ref = s16[1040,128]{1,0:T(8,128)(2,1)S(1)} collective-permute-done((s16[1040,128]{1,0:T(8,128)(2,1)S(1)}, s16[1040,128]{1,0:T(8,128)(2,1)S(1)}, u32[]{:S(2)}, u32[]{:S(2)}) %collective-permute-start.17) | collective-permute-done | bytes 266272 | tf_op jit(solution)/shard_map/ppermute | solution.py:378
  66.2 1.8 %collective-permute-start.23 = (s16[272,128]{1,0:T(8,128)(2,1)S(1)}, s16[272,128]{1,0:T(8,128)(2,1)S(1)}, u32[]{:S(2)}, u32[]{:S(2)}) collective-permute-start(s16[272,128]{1,0:T(8,128)(2,1)S(1)} %get-tuple-element.106), channel_id=1, source_target_pairs={{0,8},{1,9},{2,10},{3,11},{4,12},{5,13},{6,14},{7,15},{8,0},{9,1},... | collective-permute-start | bytes 208904 | tf_op jit(solution)/shard_map/ppermute | solution.py:378
  68.0 1.9 %collective-permute-done.19.a_ref = s16[1040,128]{1,0:T(8,128)(2,1)S(1)} collective-permute-done((s16[1040,128]{1,0:T(8,128)(2,1)S(1)}, s16[1040,128]{1,0:T(8,128)(2,1)S(1)}, u32[]{:S(2)}, u32[]{:S(2)}) %collective-permute-start.19) | collective-permute-done | bytes 266272 | tf_op jit(solution)/shard_map/ppermute | solution.py:378
  70.0 1.7 %collective-permute-start.28 = (f32[2,64,128]{2,1,0:T(8,128)S(1)}, f32[2,64,128]{2,1,0:T(8,128)S(1)}, u32[]{:S(2)}, u32[]{:S(2)}) collective-permute-start(f32[2,64,128]{2,1,0:T(8,128)S(1)} %folded.12.a_ref), channel_id=1, source_target_pairs={{0,128},{16,144},{32,160},{48,176},{64,192},{80,208},{96,224},{112... | collective-permute-start | bytes 196616 | tf_op jit(solution)/shard_map/ppermute | solution.py:413
  72.0 2.3 %collective-permute-done.24.refs_3_ = s16[272,128]{1,0:T(8,128)(2,1)S(1)} collective-permute-done((s16[272,128]{1,0:T(8,128)(2,1)S(1)}, s16[272,128]{1,0:T(8,128)(2,1)S(1)}, u32[]{:S(2)}, u32[]{:S(2)}) %collective-permute-start.24) | collective-permute-done | bytes 69664 | tf_op jit(solution)/shard_map/ppermute | solution.py:378
  74.8 3.9 %collective-permute-done.28.b_ref = f32[2,64,128]{2,1,0:T(8,128)S(1)} collective-permute-done((f32[2,64,128]{2,1,0:T(8,128)S(1)}, f32[2,64,128]{2,1,0:T(8,128)S(1)}, u32[]{:S(2)}, u32[]{:S(2)}) %collective-permute-start.28) | collective-permute-done | bytes 65568 | tf_op jit(solution)/shard_map/ppermute | solution.py:413
  79.4 2.4 %collective-permute-start.26 = (s16[272,128]{1,0:T(8,128)(2,1)S(1)}, s16[272,128]{1,0:T(8,128)(2,1)S(1)}, u32[]{:S(2)}, u32[]{:S(2)}) collective-permute-start(s16[272,128]{1,0:T(8,128)(2,1)S(1)} %get-tuple-element.116), channel_id=1, source_target_pairs={{0,2},{1,3},{2,0},{3,1},{4,6},{5,7},{6,4},{7,5},{8,10},{9,11},{10,... | collective-permute-start | bytes 208904 | tf_op jit(solution)/shard_map/ppermute | solution.py:378
  81.7 2.1 %collective-permute-start.27 = (s16[272,128]{1,0:T(8,128)(2,1)S(1)}, s16[272,128]{1,0:T(8,128)(2,1)S(1)}, u32[]{:S(2)}, u32[]{:S(2)}) collective-permute-start(s16[272,128]{1,0:T(8,128)(2,1)S(1)} %get-tuple-element.117), channel_id=1, source_target_pairs={{0,3},{1,0},{2,1},{3,2},{4,7},{5,4},{6,5},{7,6},{8,11},{9,8},{10,9... | collective-permute-start | bytes 208904 | tf_op jit(solution)/shard_map/ppermute | solution.py:378
  83.8 4.3 %inverted.1.refs_8_ = f32[128,128]{1,0:T(8,128)S(1)} custom-call(f32[64,128]{1,0:T(8,128)S(1)} %folded.13.mine_ref, f32[64,128]{1,0:T(8,128)S(1)} %collective-permute-done.29.other_ref), custom_call_target="tpu_custom_call" | custom-call | flops 4000000000 | bytes 15000000 | tf_op jit(solution)/shard_map/inverted/pallas_call | solution.py:356
  88.1 1.3 %finish.1 = f32[512,128]{1,0:T(8,128)} custom-call(f32[128,256]{1,0:T(8,128)S(1)} %get-tuple-element.101.after_ref.refs_0_, s16[272,128]{1,0:T(8,128)(2,1)S(1)} %collective-permute-done.22.refs_1_, s16[272,128]{1,0:T(8,128)(2,1)S(1)} %collective-permute-done.23.refs_2_, s16[272,128]{1,0:T(8,128)(2,1)S(1)} %collective-permute-done.24.refs_3_, ...), custom_call_target="tpu_custom_call" | custom-call | tf_op jit(solution)/shard_map/finish/pallas_call | solution.py:264
  (59 shorter events, 8.1 us)
Async XLA Ops:
  0.0 6.0 %copy-start.3 = (s32[512,128]{1,0:T(8,128)S(1)}, s32[512,128]{1,0:T(8,128)}, u32[]{:S(2)}) copy-start(s32[512,128]{1,0:T(8,128)} %u_ref.7) | copy-start | bytes 786436
  0.0 6.0 %copy-start.2 = (f32[512,128]{1,0:T(8,128)S(1)}, f32[512,128]{1,0:T(8,128)}, u32[]{:S(2)}) copy-start(f32[512,128]{1,0:T(8,128)} %v_ref.7) | copy-start | bytes 786436
  0.0 2.2 %collective-permute-start = (bf16[256,128]{1,0:T(8,128)(2,1)}, bf16[256,128]{1,0:T(8,128)(2,1)S(1)}, u32[]{:S(2)}, u32[]{:S(2)}) collective-permute-start(bf16[256,128]{1,0:T(8,128)(2,1)} %param.12), channel_id=1, source_target_pairs={{0,16},{16,0},{32,48},{48,32},{64,80},{80,64},{96,112},{112,96},{1... | collective-permute-start | bytes 196616 | tf_op jit(solution)/shard_map/ppermute | solution.py:386
  0.0 2.2 %collective-permute-start.1 = (bf16[256,128]{1,0:T(8,128)(2,1)}, bf16[256,128]{1,0:T(8,128)(2,1)S(1)}, u32[]{:S(2)}, u32[]{:S(2)}) collective-permute-start(bf16[256,128]{1,0:T(8,128)(2,1)} %param.13), channel_id=1, source_target_pairs={{0,16},{16,0},{32,48},{48,32},{64,80},{80,64},{96,112},{112,96},{1... | collective-permute-start | bytes 196616 | tf_op jit(solution)/shard_map/ppermute | solution.py:386
  2.6 7.3 %collective-permute-start.2 = (bf16[1024,128]{1,0:T(8,128)(2,1)S(1)}, bf16[1024,128]{1,0:T(8,128)(2,1)S(1)}, u32[]{:S(2)}, u32[]{:S(2)}) collective-permute-start(bf16[1024,128]{1,0:T(8,128)(2,1)S(1)} %constant_dynamic-update-slice_fusion.after_ref.refs_0_.refs_3_), channel_id=1, source_target_pairs={{0,32},{32,64},{64,96},{96,128},{128,160},{160,192},{192,224},{224... | collective-permute-start | bytes 786440 | tf_op jit(solution)/shard_map/ppermute | solution.py:390
  4.5 5.3 %collective-permute-start.3 = (f32[2,64,128]{2,1,0:T(8,128)S(1)}, f32[2,64,128]{2,1,0:T(8,128)S(1)}, u32[]{:S(2)}, u32[]{:S(2)}) collective-permute-start(f32[2,64,128]{2,1,0:T(8,128)S(1)} %partial_grams.1.a_ref), channel_id=1, source_target_pairs={{0,1},{1,0},{2,3},{3,2},{4,5},{5,4},{6,7},{7,6},{8,9},{9,8},{10,11... | collective-permute-start | bytes 196616 | tf_op jit(solution)/shard_map/ppermute | solution.py:392
  9.9 30.1 %collective-permute-start.10 = (bf16[1024,128]{1,0:T(8,128)(2,1)S(1)}, bf16[1024,128]{1,0:T(8,128)(2,1)S(1)}, u32[]{:S(2)}, u32[]{:S(2)}) collective-permute-start(bf16[1024,128]{1,0:T(8,128)(2,1)S(1)} %collective-permute-done.2.after_ref.refs_4_), channel_id=1, source_target_pairs={{0,16},{16,0},{32,48},{48,32},{64,80},{80,64},{96,112},{112,96},{1... | collective-permute-start | bytes 786440 | tf_op jit(solution)/shard_map/ppermute | solution.py:400
  10.0 8.5 %collective-permute-start.4 = (bf16[1024,128]{1,0:T(8,128)(2,1)S(1)}, bf16[1024,128]{1,0:T(8,128)(2,1)S(1)}, u32[]{:S(2)}, u32[]{:S(2)}) collective-permute-start(bf16[1024,128]{1,0:T(8,128)(2,1)S(1)} %collective-permute-done.2.after_ref.refs_4_), channel_id=1, source_target_pairs={{0,32},{32,64},{64,96},{96,128},{128,160},{160,192},{192,224},{224... | collective-permute-start | bytes 786440 | tf_op jit(solution)/shard_map/ppermute | solution.py:390
  12.0 6.5 %collective-permute-start.5 = (f32[2,64,128]{2,1,0:T(8,128)S(1)}, f32[2,64,128]{2,1,0:T(8,128)S(1)}, u32[]{:S(2)}, u32[]{:S(2)}) collective-permute-start(f32[2,64,128]{2,1,0:T(8,128)S(1)} %folded.7.a_ref), channel_id=1, source_target_pairs={{0,2},{1,3},{2,0},{3,1},{4,6},{5,7},{6,4},{7,5},{8,10},{9,11},{10,... | collective-permute-start | bytes 196616 | tf_op jit(solution)/shard_map/ppermute | solution.py:392
  18.5 21.4 %collective-permute-start.11 = (bf16[1024,128]{1,0:T(8,128)(2,1)S(1)}, bf16[1024,128]{1,0:T(8,128)(2,1)S(1)}, u32[]{:S(2)}, u32[]{:S(2)}) collective-permute-start(bf16[1024,128]{1,0:T(8,128)(2,1)S(1)} %collective-permute-done.4.after_ref.refs_5_), channel_id=1, source_target_pairs={{0,16},{16,0},{32,48},{48,32},{64,80},{80,64},{96,112},{112,96},{1... | collective-permute-start | bytes 786440 | tf_op jit(solution)/shard_map/ppermute | solution.py:400
  19.8 7.5 %collective-permute-start.6 = (bf16[1024,128]{1,0:T(8,128)(2,1)S(1)}, bf16[1024,128]{1,0:T(8,128)(2,1)S(1)}, u32[]{:S(2)}, u32[]{:S(2)}) collective-permute-start(bf16[1024,128]{1,0:T(8,128)(2,1)S(1)} %collective-permute-done.4.after_ref.refs_5_), channel_id=1, source_target_pairs={{0,32},{32,64},{64,96},{96,128},{128,160},{160,192},{192,224},{224... | collective-permute-start | bytes 786440 | tf_op jit(solution)/shard_map/ppermute | solution.py:390
  21.8 5.5 %collective-permute-start.7 = (f32[2,64,128]{2,1,0:T(8,128)S(1)}, f32[2,64,128]{2,1,0:T(8,128)S(1)}, u32[]{:S(2)}, u32[]{:S(2)}) collective-permute-start(f32[2,64,128]{2,1,0:T(8,128)S(1)} %folded.8.a_ref), channel_id=1, source_target_pairs={{0,4},{1,5},{2,6},{3,7},{4,0},{5,1},{6,2},{7,3},{8,12},{9,13},{10,... | collective-permute-start | bytes 196616 | tf_op jit(solution)/shard_map/ppermute | solution.py:392
  27.4 14.7 %collective-permute-start.12 = (bf16[1024,128]{1,0:T(8,128)(2,1)S(1)}, bf16[1024,128]{1,0:T(8,128)(2,1)S(1)}, u32[]{:S(2)}, u32[]{:S(2)}) collective-permute-start(bf16[1024,128]{1,0:T(8,128)(2,1)S(1)} %collective-permute-done.6.after_ref.refs_6_), channel_id=1, source_target_pairs={{0,16},{16,0},{32,48},{48,32},{64,80},{80,64},{96,112},{112,96},{1... | collective-permute-start | bytes 786440 | tf_op jit(solution)/shard_map/ppermute | solution.py:400
  27.5 9.1 %collective-permute-start.9 = (f32[2,64,128]{2,1,0:T(8,128)S(1)}, f32[2,64,128]{2,1,0:T(8,128)S(1)}, u32[]{:S(2)}, u32[]{:S(2)}) collective-permute-start(f32[2,64,128]{2,1,0:T(8,128)S(1)} %folded.9.a_ref), channel_id=1, source_target_pairs={{0,8},{1,9},{2,10},{3,11},{4,12},{5,13},{6,14},{7,15},{8,0},{9,1},... | collective-permute-start | bytes 196616 | tf_op jit(solution)/shard_map/ppermute | solution.py:392
  30.5 6.1 %collective-permute-start.8 = (bf16[512,128]{1,0:T(8,128)(2,1)S(1)}, bf16[512,128]{1,0:T(8,128)(2,1)S(1)}, u32[]{:S(2)}, u32[]{:S(2)}) collective-permute-start(bf16[512,128]{1,0:T(8,128)(2,1)S(1)} %slice.3), channel_id=1, source_target_pairs={{0,32},{32,64},{64,96},{96,128},{128,160},{160,192},{192,224},{224... | collective-permute-start | bytes 393224 | tf_op jit(solution)/shard_map/ppermute | solution.py:390
  36.6 5.5 %collective-permute-start.13 = (bf16[512,128]{1,0:T(8,128)(2,1)S(1)}, bf16[512,128]{1,0:T(8,128)(2,1)S(1)}, u32[]{:S(2)}, u32[]{:S(2)}) collective-permute-start(bf16[512,128]{1,0:T(8,128)(2,1)S(1)} %collective-permute-done.8.refs_7_), channel_id=1, source_target_pairs={{0,16},{16,0},{32,48},{48,32},{64,80},{80,64},{96,112},{112,96},{1... | collective-permute-start | bytes 393224 | tf_op jit(solution)/shard_map/ppermute | solution.py:400
  36.7 5.4 %collective-permute-start.14 = (f32[2,64,128]{2,1,0:T(8,128)S(1)}, f32[2,64,128]{2,1,0:T(8,128)S(1)}, u32[]{:S(2)}, u32[]{:S(2)}) collective-permute-start(f32[2,64,128]{2,1,0:T(8,128)S(1)} %folded.10.a_ref), channel_id=1, source_target_pairs={{0,32},{16,48},{32,0},{48,16},{64,96},{80,112},{96,64},{112,80},{1... | collective-permute-start | bytes 196616 | tf_op jit(solution)/shard_map/ppermute | solution.py:399
  45.7 15.2 %collective-permute-start.15 = (s16[1040,128]{1,0:T(8,128)(2,1)S(1)}, s16[1040,128]{1,0:T(8,128)(2,1)S(1)}, u32[]{:S(2)}, u32[]{:S(2)}) collective-permute-start(s16[1040,128]{1,0:T(8,128)(2,1)S(1)} %get-tuple-element.92), channel_id=1, source_target_pairs={{0,1},{1,2},{2,3},{3,0},{4,5},{5,6},{6,7},{7,4},{8,9},{9,10},{10,1... | collective-permute-start | bytes 798728 | tf_op jit(solution)/shard_map/ppermute | solution.py:378
  48.3 7.6 %collective-permute-start.18 = (f32[2,64,128]{2,1,0:T(8,128)S(1)}, f32[2,64,128]{2,1,0:T(8,128)S(1)}, u32[]{:S(2)}, u32[]{:S(2)}) collective-permute-start(f32[2,64,128]{2,1,0:T(8,128)S(1)} %folded.11.a_ref), channel_id=1, source_target_pairs={{0,64},{16,80},{32,96},{48,112},{64,0},{80,16},{96,32},{112,48},{1... | collective-permute-start | bytes 196616 | tf_op jit(solution)/shard_map/ppermute | solution.py:408
  51.0 11.0 %collective-permute-start.16 = (s16[1040,128]{1,0:T(8,128)(2,1)S(1)}, s16[1040,128]{1,0:T(8,128)(2,1)S(1)}, u32[]{:S(2)}, u32[]{:S(2)}) collective-permute-start(s16[1040,128]{1,0:T(8,128)(2,1)S(1)} %get-tuple-element.93), channel_id=1, source_target_pairs={{0,2},{1,3},{2,0},{3,1},{4,6},{5,7},{6,4},{7,5},{8,10},{9,11},{10,... | collective-permute-start | bytes 798728 | tf_op jit(solution)/shard_map/ppermute | solution.py:378
  53.8 11.2 %collective-permute-start.17 = (s16[1040,128]{1,0:T(8,128)(2,1)S(1)}, s16[1040,128]{1,0:T(8,128)(2,1)S(1)}, u32[]{:S(2)}, u32[]{:S(2)}) collective-permute-start(s16[1040,128]{1,0:T(8,128)(2,1)S(1)} %get-tuple-element.94), channel_id=1, source_target_pairs={{0,3},{1,0},{2,1},{3,2},{4,7},{5,4},{6,5},{7,6},{8,11},{9,8},{10,9... | collective-permute-start | bytes 798728 | tf_op jit(solution)/shard_map/ppermute | solution.py:378
  55.2 14.7 %collective-permute-start.19 = (s16[1040,128]{1,0:T(8,128)(2,1)S(1)}, s16[1040,128]{1,0:T(8,128)(2,1)S(1)}, u32[]{:S(2)}, u32[]{:S(2)}) collective-permute-start(s16[1040,128]{1,0:T(8,128)(2,1)S(1)} %get-tuple-element.102), channel_id=1, source_target_pairs={{0,4},{1,5},{2,6},{3,7},{4,8},{5,9},{6,10},{7,11},{8,12},{9,13},{1... | collective-permute-start | bytes 798728 | tf_op jit(solution)/shard_map/ppermute | solution.py:378
  55.9 14.1 %collective-permute-start.20 = (s16[1040,128]{1,0:T(8,128)(2,1)S(1)}, s16[1040,128]{1,0:T(8,128)(2,1)S(1)}, u32[]{:S(2)}, u32[]{:S(2)}) collective-permute-start(s16[1040,128]{1,0:T(8,128)(2,1)S(1)} %get-tuple-element.103), channel_id=1, source_target_pairs={{0,8},{1,9},{2,10},{3,11},{4,12},{5,13},{6,14},{7,15},{8,0},{9,1},... | collective-permute-start | bytes 798728 | tf_op jit(solution)/shard_map/ppermute | solution.py:378
  61.0 10.7 %collective-permute-start.21 = (s16[1040,128]{1,0:T(8,128)(2,1)S(1)}, s16[1040,128]{1,0:T(8,128)(2,1)S(1)}, u32[]{:S(2)}, u32[]{:S(2)}) collective-permute-start(s16[1040,128]{1,0:T(8,128)(2,1)S(1)} %get-tuple-element.104), channel_id=1, source_target_pairs={{0,12},{1,13},{2,14},{3,15},{4,0},{5,1},{6,2},{7,3},{8,4},{9,5},{1... | collective-permute-start | bytes 798728 | tf_op jit(solution)/shard_map/ppermute | solution.py:378
  65.5 6.2 %collective-permute-start.22 = (s16[272,128]{1,0:T(8,128)(2,1)S(1)}, s16[272,128]{1,0:T(8,128)(2,1)S(1)}, u32[]{:S(2)}, u32[]{:S(2)}) collective-permute-start(s16[272,128]{1,0:T(8,128)(2,1)S(1)} %get-tuple-element.105), channel_id=1, source_target_pairs={{0,4},{1,5},{2,6},{3,7},{4,8},{5,9},{6,10},{7,11},{8,12},{9,13},{1... | collective-permute-start | bytes 208904 | tf_op jit(solution)/shard_map/ppermute | solution.py:378
  66.2 5.8 %collective-permute-start.23 = (s16[272,128]{1,0:T(8,128)(2,1)S(1)}, s16[272,128]{1,0:T(8,128)(2,1)S(1)}, u32[]{:S(2)}, u32[]{:S(2)}) collective-permute-start(s16[272,128]{1,0:T(8,128)(2,1)S(1)} %get-tuple-element.106), channel_id=1, source_target_pairs={{0,8},{1,9},{2,10},{3,11},{4,12},{5,13},{6,14},{7,15},{8,0},{9,1},... | collective-permute-start | bytes 208904 | tf_op jit(solution)/shard_map/ppermute | solution.py:378
  69.9 4.3 %collective-permute-start.24 = (s16[272,128]{1,0:T(8,128)(2,1)S(1)}, s16[272,128]{1,0:T(8,128)(2,1)S(1)}, u32[]{:S(2)}, u32[]{:S(2)}) collective-permute-start(s16[272,128]{1,0:T(8,128)(2,1)S(1)} %get-tuple-element.107), channel_id=1, source_target_pairs={{0,12},{1,13},{2,14},{3,15},{4,0},{5,1},{6,2},{7,3},{8,4},{9,5},{1... | collective-permute-start | bytes 208904 | tf_op jit(solution)/shard_map/ppermute | solution.py:378
  70.0 8.7 %collective-permute-start.28 = (f32[2,64,128]{2,1,0:T(8,128)S(1)}, f32[2,64,128]{2,1,0:T(8,128)S(1)}, u32[]{:S(2)}, u32[]{:S(2)}) collective-permute-start(f32[2,64,128]{2,1,0:T(8,128)S(1)} %folded.12.a_ref), channel_id=1, source_target_pairs={{0,128},{16,144},{32,160},{48,176},{64,192},{80,208},{96,224},{112... | collective-permute-start | bytes 196616 | tf_op jit(solution)/shard_map/ppermute | solution.py:413
  78.7 5.1 %collective-permute-start.29 = (f32[64,128]{1,0:T(8,128)S(1)}, f32[64,128]{1,0:T(8,128)S(1)}, u32[]{:S(2)}, u32[]{:S(2)}) collective-permute-start(f32[64,128]{1,0:T(8,128)S(1)} %folded.13.mine_ref), channel_id=1, source_target_pairs={{0,16},{16,0},{32,48},{48,32},{64,80},{80,64},{96,112},{112,96},{1... | collective-permute-start | bytes 98312 | tf_op jit(solution)/shard_map/ppermute | solution.py:419
  79.0 9.0 %collective-permute-start.25 = (s16[272,128]{1,0:T(8,128)(2,1)S(1)}, s16[272,128]{1,0:T(8,128)(2,1)S(1)}, u32[]{:S(2)}, u32[]{:S(2)}) collective-permute-start(s16[272,128]{1,0:T(8,128)(2,1)S(1)} %get-tuple-element.115), channel_id=1, source_target_pairs={{0,1},{1,2},{2,3},{3,0},{4,5},{5,6},{6,7},{7,4},{8,9},{9,10},{10,1... | collective-permute-start | bytes 208904 | tf_op jit(solution)/shard_map/ppermute | solution.py:378
  79.4 8.7 %collective-permute-start.26 = (s16[272,128]{1,0:T(8,128)(2,1)S(1)}, s16[272,128]{1,0:T(8,128)(2,1)S(1)}, u32[]{:S(2)}, u32[]{:S(2)}) collective-permute-start(s16[272,128]{1,0:T(8,128)(2,1)S(1)} %get-tuple-element.116), channel_id=1, source_target_pairs={{0,2},{1,3},{2,0},{3,1},{4,6},{5,7},{6,4},{7,5},{8,10},{9,11},{10,... | collective-permute-start | bytes 208904 | tf_op jit(solution)/shard_map/ppermute | solution.py:378
  81.7 6.4 %collective-permute-start.27 = (s16[272,128]{1,0:T(8,128)(2,1)S(1)}, s16[272,128]{1,0:T(8,128)(2,1)S(1)}, u32[]{:S(2)}, u32[]{:S(2)}) collective-permute-start(s16[272,128]{1,0:T(8,128)(2,1)S(1)} %get-tuple-element.117), channel_id=1, source_target_pairs={{0,3},{1,0},{2,1},{3,2},{4,7},{5,4},{6,5},{7,6},{8,11},{9,8},{10,9... | collective-permute-start | bytes 208904 | tf_op jit(solution)/shard_map/ppermute | solution.py:378
  (2 other events, 11.1 us)

commit v2 on v0

--- a/solution.py
+++ b/solution.py
@@ -19,7 +19,7 @@
 EXTRA = 16
 PARTS = 4
 SLICES = 2
-PIVOTS = 4
+PIVOTS = 8
 SLICE = RANK // SLICES
 SIDE = 4
 TILES_OWN = OWN // LO
@@ -396,9 +396,12 @@
             arriving, low, grams = after((arriving, low, grams))
             more = lax.ppermute(grams, "cols", swapped(2))
         else:
-            grams = folded(found[-1], grams, more)
+            grams = folded(low if step == 1 else found[-1], grams, more)
             more = lax.ppermute(grams, *(("cols", swapped(2 << step)) if step < 3 else ("rows", swapped(2))))
-            arriving, low, more = after((arriving, low, more))
+            if step == 1:
+                arriving, low = after((arriving, low))
+            else:
+                arriving, low, more = after((arriving, low, more))
         highs.append(high)
         lows.append(low)
         found.append(arriving)

time: 86.5 us -> 85.3 us (0.986)
  waiting for transfers between devices: 12.7 us -> 11 us
  starting transfers between devices: 42.9 us -> 44.1 us
    ppermute x4, starting transfers between devices: 8.24 us -> 10.8 us  [on_device(): lax.ppermute(found[-1] if step < 3 else found[-1][:2 * ROWS], 'rows', aro...]
    ppermute x1, waiting for transfers between devices: 1.12 us -> 0.01 us  [on_device(): more = lax.ppermute(grams, 'cols', swapped(2))]
  transfers between devices with their start and end apart: 30 -> 30, of which waited for: 7 -> 6; matrix products, arithmetic and copies ran while one was open for 2% -> 2% of each run, Pallas kernels for 26% -> 26%
where the time goes in v2:
time: 85.3 us; the launch traced here: 85.2 us
  starting transfers between devices  44.1 us (52%)
  Pallas kernels  27.3 us (32%)
  waiting for transfers between devices  11 us (13%)
  local copies, waits for them, and re-layouts  1.75 us (2%)
  between operations  0.96 us (1%)
    ppermute x12, starting transfers between devices, along(): lax.ppermute(xs[k - 1], 'cols', moved(k))  18.1 us
    pallas_call x4, Pallas kernels, build_weights(): pl.pallas_call(functools.partial(build_body, block=block), grid=(1,), in_...  15 us
    ppermute x4, starting transfers between devices, on_device(): lax.ppermute(found[-1] if step < 3 else found[-1][:2 * ROWS], 'rows', aro...  10.8 us
    ppermute x12, waiting for transfers between devices, along(): lax.ppermute(xs[k - 1], 'cols', moved(k))  6.87 us
    pallas_call x2, Pallas kernels, products(): pl.pallas_call(functools.partial(product_body, along_x=along_x, sizes=siz...  5.54 us
    ppermute x3, starting transfers between devices, on_device(): lax.ppermute(grams, *(('cols', swapped(2 << step)) if step < 3 else ('row...  5.53 us
    pallas_call x1, Pallas kernels, inverted(): pl.pallas_call(functools.partial(inverse_body, me=me), in_specs=[in_vmem,...  4 us
    ppermute x1, waiting for transfers between devices, on_device(): more = lax.ppermute(grams, 'rows', swapped(4))  2.98 us
  transfers between devices with their start and end apart: 30, of which 6 were waited for; matrix products, arithmetic and copies ran while one was open for 2% of the time, Pallas kernels for 26%

profile of v2, /device:TPU:32, one launch (start us, length us, event | category | flops | bytes accessed | tf_op | source)
XLA Modules:
  0.0 85.2 jit_solution(1291949554188774536)
XLA Ops:
  2.6 2.0 %collective-permute-start.2 = (bf16[1024,128]{1,0:T(8,128)(2,1)S(1)}, bf16[1024,128]{1,0:T(8,128)(2,1)S(1)}, u32[]{:S(2)}, u32[]{:S(2)}) collective-permute-start(bf16[1024,128]{1,0:T(8,128)(2,1)S(1)} %constant_dynamic-update-slice_fusion.after_ref.refs_0_.refs_3_), channel_id=1, source_target_pairs={{0,32},{32,64},{64,96},{96,128},{128,160},{160,192},{192,224},{224... | collective-permute-start | bytes 786440 | tf_op jit(solution)/shard_map/ppermute | solution.py:392
  4.5 1.5 %collective-permute-start.3 = (f32[2,64,128]{2,1,0:T(8,128)S(1)}, f32[2,64,128]{2,1,0:T(8,128)S(1)}, u32[]{:S(2)}, u32[]{:S(2)}) collective-permute-start(f32[2,64,128]{2,1,0:T(8,128)S(1)} %partial_grams.1.a_ref), channel_id=1, source_target_pairs={{0,1},{1,0},{2,3},{3,2},{4,5},{5,4},{6,7},{7,6},{8,9},{9,8},{10,11... | collective-permute-start | bytes 196616 | tf_op jit(solution)/shard_map/ppermute | solution.py:390
  6.0 3.8 %build_weights.4 = (bf16[64,128,128]{2,1,0:T(8,128)(2,1)S(1)}, bf16[64,128,128]{2,1,0:T(8,128)(2,1)S(1)}) custom-call(f32[512,128]{1,0:T(8,128)S(1)} %copy-done.2, s32[512,128]{1,0:T(8,128)S(1)} %copy-done.3, bf16[1024,128]{1,0:T(8,128)(2,1)S(1)} %constant_dynamic-update-slice_fusion.after_ref.refs_0_.refs_3_), custom_call_target="tpu_custom_call" | custom-call | flops 6000000000 | bytes 20000000 | tf_op jit(solution)/shard_map/build_weights/pallas_call | solution.py:71
  9.9 2.8 %collective-permute-start.6 = (f32[2,64,128]{2,1,0:T(8,128)S(1)}, f32[2,64,128]{2,1,0:T(8,128)S(1)}, u32[]{:S(2)}, u32[]{:S(2)}) collective-permute-start(f32[2,64,128]{2,1,0:T(8,128)S(1)} %folded.7.a_ref), channel_id=1, source_target_pairs={{0,2},{1,3},{2,0},{3,1},{4,6},{5,7},{6,4},{7,5},{8,10},{9,11},{10,... | collective-permute-start | bytes 196616 | tf_op jit(solution)/shard_map/ppermute | solution.py:397
  12.7 1.9 %collective-permute-start.4 = (bf16[1024,128]{1,0:T(8,128)(2,1)S(1)}, bf16[1024,128]{1,0:T(8,128)(2,1)S(1)}, u32[]{:S(2)}, u32[]{:S(2)}) collective-permute-start(bf16[1024,128]{1,0:T(8,128)(2,1)S(1)} %collective-permute-done.2.after_ref.refs_4_), channel_id=1, source_target_pairs={{0,32},{32,64},{64,96},{96,128},{128,160},{160,192},{192,224},{224... | collective-permute-start | bytes 786440 | tf_op jit(solution)/shard_map/ppermute | solution.py:392
  14.7 3.7 %build_weights.5 = (bf16[64,128,128]{2,1,0:T(8,128)(2,1)S(1)}, bf16[64,128,128]{2,1,0:T(8,128)(2,1)S(1)}) custom-call(f32[512,128]{1,0:T(8,128)S(1)} %copy-done.2, s32[512,128]{1,0:T(8,128)S(1)} %copy-done.3, bf16[1024,128]{1,0:T(8,128)(2,1)S(1)} %collective-permute-done.2.after_ref.refs_4_), custom_call_target="tpu_custom_call" | custom-call | flops 6000000000 | bytes 20000000 | tf_op jit(solution)/shard_map/build_weights/pallas_call | solution.py:71
  18.4 1.7 %collective-permute-start.7 = (f32[2,64,128]{2,1,0:T(8,128)S(1)}, f32[2,64,128]{2,1,0:T(8,128)S(1)}, u32[]{:S(2)}, u32[]{:S(2)}) collective-permute-start(f32[2,64,128]{2,1,0:T(8,128)S(1)} %folded.8.a_ref), channel_id=1, source_target_pairs={{0,4},{1,5},{2,6},{3,7},{4,0},{5,1},{6,2},{7,3},{8,12},{9,13},{10,... | collective-permute-start | bytes 196616 | tf_op jit(solution)/shard_map/ppermute | solution.py:400
  20.9 2.8 %collective-permute-start.5 = (bf16[1024,128]{1,0:T(8,128)(2,1)S(1)}, bf16[1024,128]{1,0:T(8,128)(2,1)S(1)}, u32[]{:S(2)}, u32[]{:S(2)}) collective-permute-start(bf16[1024,128]{1,0:T(8,128)(2,1)S(1)} %collective-permute-done.4.after_ref.refs_5_), channel_id=1, source_target_pairs={{0,32},{32,64},{64,96},{96,128},{128,160},{160,192},{192,224},{224... | collective-permute-start | bytes 786440 | tf_op jit(solution)/shard_map/ppermute | solution.py:392
  23.7 3.0 %collective-permute-start.8 = (f32[2,64,128]{2,1,0:T(8,128)S(1)}, f32[2,64,128]{2,1,0:T(8,128)S(1)}, u32[]{:S(2)}, u32[]{:S(2)}) collective-permute-start(f32[2,64,128]{2,1,0:T(8,128)S(1)} %folded.9.a_ref), channel_id=1, source_target_pairs={{0,8},{1,9},{2,10},{3,11},{4,12},{5,13},{6,14},{7,15},{8,0},{9,1},... | collective-permute-start | bytes 196616 | tf_op jit(solution)/shard_map/ppermute | solution.py:400
  26.7 3.7 %build_weights.6 = (bf16[64,128,128]{2,1,0:T(8,128)(2,1)S(1)}, bf16[64,128,128]{2,1,0:T(8,128)(2,1)S(1)}) custom-call(f32[512,128]{1,0:T(8,128)S(1)} %copy-done.2, s32[512,128]{1,0:T(8,128)S(1)} %copy-done.3, bf16[1024,128]{1,0:T(8,128)(2,1)S(1)} %collective-permute-done.4.after_ref.refs_5_), custom_call_target="tpu_custom_call" | custom-call | flops 6000000000 | bytes 20000000 | tf_op jit(solution)/shard_map/build_weights/pallas_call | solution.py:71
  30.7 0.9 %collective-permute-start.10 = (f32[2,64,128]{2,1,0:T(8,128)S(1)}, f32[2,64,128]{2,1,0:T(8,128)S(1)}, u32[]{:S(2)}, u32[]{:S(2)}) collective-permute-start(f32[2,64,128]{2,1,0:T(8,128)S(1)} %folded.10.a_ref), channel_id=1, source_target_pairs={{0,32},{16,48},{32,0},{48,16},{64,96},{80,112},{96,64},{112,80},{1... | collective-permute-start | bytes 196616 | tf_op jit(solution)/shard_map/ppermute | solution.py:400
  31.6 4.1 %collective-permute-start.9 = (bf16[512,128]{1,0:T(8,128)(2,1)S(1)}, bf16[512,128]{1,0:T(8,128)(2,1)S(1)}, u32[]{:S(2)}, u32[]{:S(2)}) collective-permute-start(bf16[512,128]{1,0:T(8,128)(2,1)S(1)} %slice.3), channel_id=1, source_target_pairs={{0,32},{32,64},{64,96},{96,128},{128,160},{160,192},{192,224},{224... | collective-permute-start | bytes 393224 | tf_op jit(solution)/shard_map/ppermute | solution.py:392
  35.7 3.8 %build_weights.7 = (bf16[64,128,128]{2,1,0:T(8,128)(2,1)S(1)}, bf16[64,128,128]{2,1,0:T(8,128)(2,1)S(1)}) custom-call(f32[512,128]{1,0:T(8,128)S(1)} %copy-done.2, s32[512,128]{1,0:T(8,128)S(1)} %copy-done.3, bf16[1024,128]{1,0:T(8,128)(2,1)S(1)} %collective-permute-done.5.after_ref.refs_6_), custom_call_target="tpu_custom_call" | custom-call | flops 6000000000 | bytes 20000000 | tf_op jit(solution)/shard_map/build_weights/pallas_call | solution.py:71
  41.1 3.7 %products.2 = (s16[1040,128]{1,0:T(8,128)(2,1)S(1)}, s16[1040,128]{1,0:T(8,128)(2,1)S(1)}, s16[1040,128]{1,0:T(8,128)(2,1)S(1)}, f32[4,128,256]{2,1,0:T(8,128)S(1)}, bf16[256,512]{1,0:T(8,128)(2,1)S(1)}) custom-call(s32[512]{0:T(512)S(1)} %copy-done, s32[512]{0:T(512)S(1)} %copy-done.1, s32[1]{0:T(128)S(6)} %copy.11.refs_2_, ...), custom_call_target="tpu_custom_call" | custom-call | flops 4000000000 | bytes 13000000 | tf_op jit(solution)/shard_map/products/pallas_call | solution.py:196
  45.5 2.0 %collective-permute-start.17 = (s16[1040,128]{1,0:T(8,128)(2,1)S(1)}, s16[1040,128]{1,0:T(8,128)(2,1)S(1)}, u32[]{:S(2)}, u32[]{:S(2)}) collective-permute-start(s16[1040,128]{1,0:T(8,128)(2,1)S(1)} %get-tuple-element.67), channel_id=1, source_target_pairs={{0,2},{1,3},{2,0},{3,1},{4,6},{5,7},{6,4},{7,5},{8,10},{9,11},{10,... | collective-permute-start | bytes 798728 | tf_op jit(solution)/shard_map/ppermute | solution.py:378
  48.3 1.9 %products.3 = (s16[1040,128]{1,0:T(8,128)(2,1)S(1)}, s16[1040,128]{1,0:T(8,128)(2,1)S(1)}, s16[1040,128]{1,0:T(8,128)(2,1)S(1)}, f32[4,128,256]{2,1,0:T(8,128)S(1)}) custom-call(bf16[256,512]{1,0:T(8,128)(2,1)S(1)} %get-tuple-element.62.refs_0_, bf16[64,128,128]{2,1,0:T(8,128)(2,1)S(1)} %get-tuple-element.53.refs_12_.refs_1_, ...), custom_call_target="tpu_custom_call" | custom-call | flops 4000000000 | bytes 13000000 | tf_op jit(solution)/shard_map/products/pallas_call | solution.py:196
  50.1 1.3 %collective-permute-start.15 = (f32[2,64,128]{2,1,0:T(8,128)S(1)}, f32[2,64,128]{2,1,0:T(8,128)S(1)}, u32[]{:S(2)}, u32[]{:S(2)}) collective-permute-start(f32[2,64,128]{2,1,0:T(8,128)S(1)} %folded.11.a_ref), channel_id=1, source_target_pairs={{0,64},{16,80},{32,96},{48,112},{64,0},{80,16},{96,32},{112,48},{1... | collective-permute-start | bytes 196616 | tf_op jit(solution)/shard_map/ppermute | solution.py:415
  51.5 0.9 %collective-permute-start.22 = (s16[1040,128]{1,0:T(8,128)(2,1)S(1)}, s16[1040,128]{1,0:T(8,128)(2,1)S(1)}, u32[]{:S(2)}, u32[]{:S(2)}) collective-permute-start(s16[1040,128]{1,0:T(8,128)(2,1)S(1)} %get-tuple-element.73), channel_id=1, source_target_pairs={{0,4},{1,5},{2,6},{3,7},{4,8},{5,9},{6,10},{7,11},{8,12},{9,13},{1... | collective-permute-start | bytes 798728 | tf_op jit(solution)/shard_map/ppermute | solution.py:378
  52.4 3.0 %collective-permute-done.15.b_ref = f32[2,64,128]{2,1,0:T(8,128)S(1)} collective-permute-done((f32[2,64,128]{2,1,0:T(8,128)S(1)}, f32[2,64,128]{2,1,0:T(8,128)S(1)}, u32[]{:S(2)}, u32[]{:S(2)}) %collective-permute-start.15) | collective-permute-done | bytes 65568 | tf_op jit(solution)/shard_map/ppermute | solution.py:415
  55.4 2.1 %collective-permute-start.23 = (s16[1040,128]{1,0:T(8,128)(2,1)S(1)}, s16[1040,128]{1,0:T(8,128)(2,1)S(1)}, u32[]{:S(2)}, u32[]{:S(2)}) collective-permute-start(s16[1040,128]{1,0:T(8,128)(2,1)S(1)} %get-tuple-element.74), channel_id=1, source_target_pairs={{0,8},{1,9},{2,10},{3,11},{4,12},{5,13},{6,14},{7,15},{8,0},{9,1},... | collective-permute-start | bytes 798728 | tf_op jit(solution)/shard_map/ppermute | solution.py:378
  57.5 2.8 %collective-permute-done.16.a_ref = s16[1040,128]{1,0:T(8,128)(2,1)S(1)} collective-permute-done((s16[1040,128]{1,0:T(8,128)(2,1)S(1)}, s16[1040,128]{1,0:T(8,128)(2,1)S(1)}, u32[]{:S(2)}, u32[]{:S(2)}) %collective-permute-start.16) | collective-permute-done | bytes 266272 | tf_op jit(solution)/shard_map/ppermute | solution.py:378
  60.2 2.1 %collective-permute-start.24 = (s16[1040,128]{1,0:T(8,128)(2,1)S(1)}, s16[1040,128]{1,0:T(8,128)(2,1)S(1)}, u32[]{:S(2)}, u32[]{:S(2)}) collective-permute-start(s16[1040,128]{1,0:T(8,128)(2,1)S(1)} %get-tuple-element.75), channel_id=1, source_target_pairs={{0,12},{1,13},{2,14},{3,15},{4,0},{5,1},{6,2},{7,3},{8,4},{9,5},{1... | collective-permute-start | bytes 798728 | tf_op jit(solution)/shard_map/ppermute | solution.py:378
  63.0 2.1 %collective-permute-start.28 = (f32[2,64,128]{2,1,0:T(8,128)S(1)}, f32[2,64,128]{2,1,0:T(8,128)S(1)}, u32[]{:S(2)}, u32[]{:S(2)}) collective-permute-start(f32[2,64,128]{2,1,0:T(8,128)S(1)} %folded.12.a_ref), channel_id=1, source_target_pairs={{0,128},{16,144},{32,160},{48,176},{64,192},{80,208},{96,224},{112... | collective-permute-start | bytes 196616 | tf_op jit(solution)/shard_map/ppermute | solution.py:420
  65.1 1.3 %collective-permute-done.23.b_ref = s16[1040,128]{1,0:T(8,128)(2,1)S(1)} collective-permute-done((s16[1040,128]{1,0:T(8,128)(2,1)S(1)}, s16[1040,128]{1,0:T(8,128)(2,1)S(1)}, u32[]{:S(2)}, u32[]{:S(2)}) %collective-permute-start.23) | collective-permute-done | bytes 266272 | tf_op jit(solution)/shard_map/ppermute | solution.py:378
  66.4 2.7 %collective-permute-done.24.c_ref = s16[1040,128]{1,0:T(8,128)(2,1)S(1)} collective-permute-done((s16[1040,128]{1,0:T(8,128)(2,1)S(1)}, s16[1040,128]{1,0:T(8,128)(2,1)S(1)}, u32[]{:S(2)}, u32[]{:S(2)}) %collective-permute-start.24) | collective-permute-done | bytes 266272 | tf_op jit(solution)/shard_map/ppermute | solution.py:378
  69.7 1.0 %collective-permute-start.25 = (s16[272,128]{1,0:T(8,128)(2,1)S(1)}, s16[272,128]{1,0:T(8,128)(2,1)S(1)}, u32[]{:S(2)}, u32[]{:S(2)}) collective-permute-start(s16[272,128]{1,0:T(8,128)(2,1)S(1)} %get-tuple-element.77), channel_id=1, source_target_pairs={{0,1},{1,2},{2,3},{3,0},{4,5},{5,6},{6,7},{7,4},{8,9},{9,10},{10,1... | collective-permute-start | bytes 208904 | tf_op jit(solution)/shard_map/ppermute | solution.py:378
  71.4 1.2 %collective-permute-start.26 = (s16[272,128]{1,0:T(8,128)(2,1)S(1)}, s16[272,128]{1,0:T(8,128)(2,1)S(1)}, u32[]{:S(2)}, u32[]{:S(2)}) collective-permute-start(s16[272,128]{1,0:T(8,128)(2,1)S(1)} %get-tuple-element.78), channel_id=1, source_target_pairs={{0,2},{1,3},{2,0},{3,1},{4,6},{5,7},{6,4},{7,5},{8,10},{9,11},{10,... | collective-permute-start | bytes 208904 | tf_op jit(solution)/shard_map/ppermute | solution.py:378
  72.5 2.6 %collective-permute-start.27 = (s16[272,128]{1,0:T(8,128)(2,1)S(1)}, s16[272,128]{1,0:T(8,128)(2,1)S(1)}, u32[]{:S(2)}, u32[]{:S(2)}) collective-permute-start(s16[272,128]{1,0:T(8,128)(2,1)S(1)} %get-tuple-element.79), channel_id=1, source_target_pairs={{0,3},{1,0},{2,1},{3,2},{4,7},{5,4},{6,5},{7,6},{8,11},{9,8},{10,9... | collective-permute-start | bytes 208904 | tf_op jit(solution)/shard_map/ppermute | solution.py:378
  75.1 1.4 %collective-permute-start.19 = (s16[272,128]{1,0:T(8,128)(2,1)S(1)}, s16[272,128]{1,0:T(8,128)(2,1)S(1)}, u32[]{:S(2)}, u32[]{:S(2)}) collective-permute-start(s16[272,128]{1,0:T(8,128)(2,1)S(1)} %get-tuple-element.70), channel_id=1, source_target_pairs={{0,4},{1,5},{2,6},{3,7},{4,8},{5,9},{6,10},{7,11},{8,12},{9,13},{1... | collective-permute-start | bytes 208904 | tf_op jit(solution)/shard_map/ppermute | solution.py:378
  76.6 2.7 %collective-permute-start.20 = (s16[272,128]{1,0:T(8,128)(2,1)S(1)}, s16[272,128]{1,0:T(8,128)(2,1)S(1)}, u32[]{:S(2)}, u32[]{:S(2)}) collective-permute-start(s16[272,128]{1,0:T(8,128)(2,1)S(1)} %get-tuple-element.71), channel_id=1, source_target_pairs={{0,8},{1,9},{2,10},{3,11},{4,12},{5,13},{6,14},{7,15},{8,0},{9,1},... | collective-permute-start | bytes 208904 | tf_op jit(solution)/shard_map/ppermute | solution.py:378
  79.8 4.0 %inverted.1.refs_8_ = f32[128,128]{1,0:T(8,128)S(1)} custom-call(f32[64,128]{1,0:T(8,128)S(1)} %folded.13.mine_ref, f32[64,128]{1,0:T(8,128)S(1)} %collective-permute-done.29.other_ref), custom_call_target="tpu_custom_call" | custom-call | flops 4000000000 | bytes 15000000 | tf_op jit(solution)/shard_map/inverted/pallas_call | solution.py:356
  83.9 1.3 %finish.1 = f32[512,128]{1,0:T(8,128)} custom-call(f32[128,256]{1,0:T(8,128)S(1)} %get-tuple-element.69.after_ref.refs_0_, s16[272,128]{1,0:T(8,128)(2,1)S(1)} %collective-permute-done.19.refs_1_, s16[272,128]{1,0:T(8,128)(2,1)S(1)} %collective-permute-done.20.refs_2_, s16[272,128]{1,0:T(8,128)(2,1)S(1)} %collective-permute-done.21.refs_3_, ...), custom_call_target="tpu_custom_call" | custom-call | tf_op jit(solution)/shard_map/finish/pallas_call | solution.py:264
  (59 shorter events, 8.4 us)
Async XLA Ops:
  0.0 2.2 %collective-permute-start = (bf16[256,128]{1,0:T(8,128)(2,1)}, bf16[256,128]{1,0:T(8,128)(2,1)S(1)}, u32[]{:S(2)}, u32[]{:S(2)}) collective-permute-start(bf16[256,128]{1,0:T(8,128)(2,1)} %param.12), channel_id=1, source_target_pairs={{0,16},{16,0},{32,48},{48,32},{64,80},{80,64},{96,112},{112,96},{1... | collective-permute-start | bytes 196616 | tf_op jit(solution)/shard_map/ppermute | solution.py:386
  0.0 2.2 %collective-permute-start.1 = (bf16[256,128]{1,0:T(8,128)(2,1)}, bf16[256,128]{1,0:T(8,128)(2,1)S(1)}, u32[]{:S(2)}, u32[]{:S(2)}) collective-permute-start(bf16[256,128]{1,0:T(8,128)(2,1)} %param.13), channel_id=1, source_target_pairs={{0,16},{16,0},{32,48},{48,32},{64,80},{80,64},{96,112},{112,96},{1... | collective-permute-start | bytes 196616 | tf_op jit(solution)/shard_map/ppermute | solution.py:386
  2.6 7.4 %collective-permute-start.2 = (bf16[1024,128]{1,0:T(8,128)(2,1)S(1)}, bf16[1024,128]{1,0:T(8,128)(2,1)S(1)}, u32[]{:S(2)}, u32[]{:S(2)}) collective-permute-start(bf16[1024,128]{1,0:T(8,128)(2,1)S(1)} %constant_dynamic-update-slice_fusion.after_ref.refs_0_.refs_3_), channel_id=1, source_target_pairs={{0,32},{32,64},{64,96},{96,128},{128,160},{160,192},{192,224},{224... | collective-permute-start | bytes 786440 | tf_op jit(solution)/shard_map/ppermute | solution.py:392
  4.5 5.3 %collective-permute-start.3 = (f32[2,64,128]{2,1,0:T(8,128)S(1)}, f32[2,64,128]{2,1,0:T(8,128)S(1)}, u32[]{:S(2)}, u32[]{:S(2)}) collective-permute-start(f32[2,64,128]{2,1,0:T(8,128)S(1)} %partial_grams.1.a_ref), channel_id=1, source_target_pairs={{0,1},{1,0},{2,3},{3,2},{4,5},{5,4},{6,7},{7,6},{8,9},{9,8},{10,11... | collective-permute-start | bytes 196616 | tf_op jit(solution)/shard_map/ppermute | solution.py:390
  9.9 8.4 %collective-permute-start.6 = (f32[2,64,128]{2,1,0:T(8,128)S(1)}, f32[2,64,128]{2,1,0:T(8,128)S(1)}, u32[]{:S(2)}, u32[]{:S(2)}) collective-permute-start(f32[2,64,128]{2,1,0:T(8,128)S(1)} %folded.7.a_ref), channel_id=1, source_target_pairs={{0,2},{1,3},{2,0},{3,1},{4,6},{5,7},{6,4},{7,5},{8,10},{9,11},{10,... | collective-permute-start | bytes 196616 | tf_op jit(solution)/shard_map/ppermute | solution.py:397
  12.7 8.1 %collective-permute-start.4 = (bf16[1024,128]{1,0:T(8,128)(2,1)S(1)}, bf16[1024,128]{1,0:T(8,128)(2,1)S(1)}, u32[]{:S(2)}, u32[]{:S(2)}) collective-permute-start(bf16[1024,128]{1,0:T(8,128)(2,1)S(1)} %collective-permute-done.2.after_ref.refs_4_), channel_id=1, source_target_pairs={{0,32},{32,64},{64,96},{96,128},{128,160},{160,192},{192,224},{224... | collective-permute-start | bytes 786440 | tf_op jit(solution)/shard_map/ppermute | solution.py:392
  18.4 5.3 %collective-permute-start.7 = (f32[2,64,128]{2,1,0:T(8,128)S(1)}, f32[2,64,128]{2,1,0:T(8,128)S(1)}, u32[]{:S(2)}, u32[]{:S(2)}) collective-permute-start(f32[2,64,128]{2,1,0:T(8,128)S(1)} %folded.8.a_ref), channel_id=1, source_target_pairs={{0,4},{1,5},{2,6},{3,7},{4,0},{5,1},{6,2},{7,3},{8,12},{9,13},{10,... | collective-permute-start | bytes 196616 | tf_op jit(solution)/shard_map/ppermute | solution.py:400
  20.0 20.4 %collective-permute-start.11 = (bf16[1024,128]{1,0:T(8,128)(2,1)S(1)}, bf16[1024,128]{1,0:T(8,128)(2,1)S(1)}, u32[]{:S(2)}, u32[]{:S(2)}) collective-permute-start(bf16[1024,128]{1,0:T(8,128)(2,1)S(1)} %collective-permute-done.2.after_ref.refs_4_), channel_id=1, source_target_pairs={{0,16},{16,0},{32,48},{48,32},{64,80},{80,64},{96,112},{112,96},{1... | collective-permute-start | bytes 786440 | tf_op jit(solution)/shard_map/ppermute | solution.py:408
  20.9 19.6 %collective-permute-start.12 = (bf16[1024,128]{1,0:T(8,128)(2,1)S(1)}, bf16[1024,128]{1,0:T(8,128)(2,1)S(1)}, u32[]{:S(2)}, u32[]{:S(2)}) collective-permute-start(bf16[1024,128]{1,0:T(8,128)(2,1)S(1)} %collective-permute-done.4.after_ref.refs_5_), channel_id=1, source_target_pairs={{0,16},{16,0},{32,48},{48,32},{64,80},{80,64},{96,112},{112,96},{1... | collective-permute-start | bytes 786440 | tf_op jit(solution)/shard_map/ppermute | solution.py:408
  20.9 9.5 %collective-permute-start.5 = (bf16[1024,128]{1,0:T(8,128)(2,1)S(1)}, bf16[1024,128]{1,0:T(8,128)(2,1)S(1)}, u32[]{:S(2)}, u32[]{:S(2)}) collective-permute-start(bf16[1024,128]{1,0:T(8,128)(2,1)S(1)} %collective-permute-done.4.after_ref.refs_5_), channel_id=1, source_target_pairs={{0,32},{32,64},{64,96},{96,128},{128,160},{160,192},{192,224},{224... | collective-permute-start | bytes 786440 | tf_op jit(solution)/shard_map/ppermute | solution.py:392
  23.7 6.7 %collective-permute-start.8 = (f32[2,64,128]{2,1,0:T(8,128)S(1)}, f32[2,64,128]{2,1,0:T(8,128)S(1)}, u32[]{:S(2)}, u32[]{:S(2)}) collective-permute-start(f32[2,64,128]{2,1,0:T(8,128)S(1)} %folded.9.a_ref), channel_id=1, source_target_pairs={{0,8},{1,9},{2,10},{3,11},{4,12},{5,13},{6,14},{7,15},{8,0},{9,1},... | collective-permute-start | bytes 196616 | tf_op jit(solution)/shard_map/ppermute | solution.py:400
  30.4 10.7 %collective-permute-start.13 = (bf16[1024,128]{1,0:T(8,128)(2,1)S(1)}, bf16[1024,128]{1,0:T(8,128)(2,1)S(1)}, u32[]{:S(2)}, u32[]{:S(2)}) collective-permute-start(bf16[1024,128]{1,0:T(8,128)(2,1)S(1)} %collective-permute-done.5.after_ref.refs_6_), channel_id=1, source_target_pairs={{0,16},{16,0},{32,48},{48,32},{64,80},{80,64},{96,112},{112,96},{1... | collective-permute-start | bytes 786440 | tf_op jit(solution)/shard_map/ppermute | solution.py:408
  30.6 10.5 %copy-start = (s32[512]{0:T(512)S(1)}, s32[512]{0:T(512)}, u32[]{:S(2)}) copy-start(s32[512]{0:T(512)} %refs_0_.1) | copy-start | bytes 6148
  30.7 10.5 %copy-start.1 = (s32[512]{0:T(512)S(1)}, s32[512]{0:T(512)}, u32[]{:S(2)}) copy-start(s32[512]{0:T(512)} %refs_1_.1) | copy-start | bytes 6148
  30.7 8.8 %collective-permute-start.10 = (f32[2,64,128]{2,1,0:T(8,128)S(1)}, f32[2,64,128]{2,1,0:T(8,128)S(1)}, u32[]{:S(2)}, u32[]{:S(2)}) collective-permute-start(f32[2,64,128]{2,1,0:T(8,128)S(1)} %folded.10.a_ref), channel_id=1, source_target_pairs={{0,32},{16,48},{32,0},{48,16},{64,96},{80,112},{96,64},{112,80},{1... | collective-permute-start | bytes 196616 | tf_op jit(solution)/shard_map/ppermute | solution.py:400
  31.6 7.9 %collective-permute-start.9 = (bf16[512,128]{1,0:T(8,128)(2,1)S(1)}, bf16[512,128]{1,0:T(8,128)(2,1)S(1)}, u32[]{:S(2)}, u32[]{:S(2)}) collective-permute-start(bf16[512,128]{1,0:T(8,128)(2,1)S(1)} %slice.3), channel_id=1, source_target_pairs={{0,32},{32,64},{64,96},{96,128},{128,160},{160,192},{192,224},{224... | collective-permute-start | bytes 393224 | tf_op jit(solution)/shard_map/ppermute | solution.py:392
  39.5 1.6 %collective-permute-start.14 = (bf16[512,128]{1,0:T(8,128)(2,1)S(1)}, bf16[512,128]{1,0:T(8,128)(2,1)S(1)}, u32[]{:S(2)}, u32[]{:S(2)}) collective-permute-start(bf16[512,128]{1,0:T(8,128)(2,1)S(1)} %collective-permute-done.9.refs_7_), channel_id=1, source_target_pairs={{0,16},{16,0},{32,48},{48,32},{64,80},{80,64},{96,112},{112,96},{1... | collective-permute-start | bytes 393224 | tf_op jit(solution)/shard_map/ppermute | solution.py:408
  44.8 15.4 %collective-permute-start.16 = (s16[1040,128]{1,0:T(8,128)(2,1)S(1)}, s16[1040,128]{1,0:T(8,128)(2,1)S(1)}, u32[]{:S(2)}, u32[]{:S(2)}) collective-permute-start(s16[1040,128]{1,0:T(8,128)(2,1)S(1)} %get-tuple-element.66), channel_id=1, source_target_pairs={{0,1},{1,2},{2,3},{3,0},{4,5},{5,6},{6,7},{7,4},{8,9},{9,10},{10,1... | collective-permute-start | bytes 798728 | tf_op jit(solution)/shard_map/ppermute | solution.py:378
  45.5 16.9 %collective-permute-start.17 = (s16[1040,128]{1,0:T(8,128)(2,1)S(1)}, s16[1040,128]{1,0:T(8,128)(2,1)S(1)}, u32[]{:S(2)}, u32[]{:S(2)}) collective-permute-start(s16[1040,128]{1,0:T(8,128)(2,1)S(1)} %get-tuple-element.67), channel_id=1, source_target_pairs={{0,2},{1,3},{2,0},{3,1},{4,6},{5,7},{6,4},{7,5},{8,10},{9,11},{10,... | collective-permute-start | bytes 798728 | tf_op jit(solution)/shard_map/ppermute | solution.py:378
  47.5 14.9 %collective-permute-start.18 = (s16[1040,128]{1,0:T(8,128)(2,1)S(1)}, s16[1040,128]{1,0:T(8,128)(2,1)S(1)}, u32[]{:S(2)}, u32[]{:S(2)}) collective-permute-start(s16[1040,128]{1,0:T(8,128)(2,1)S(1)} %get-tuple-element.68), channel_id=1, source_target_pairs={{0,3},{1,0},{2,1},{3,2},{4,7},{5,4},{6,5},{7,6},{8,11},{9,8},{10,9... | collective-permute-start | bytes 798728 | tf_op jit(solution)/shard_map/ppermute | solution.py:378
  50.1 5.3 %collective-permute-start.15 = (f32[2,64,128]{2,1,0:T(8,128)S(1)}, f32[2,64,128]{2,1,0:T(8,128)S(1)}, u32[]{:S(2)}, u32[]{:S(2)}) collective-permute-start(f32[2,64,128]{2,1,0:T(8,128)S(1)} %folded.11.a_ref), channel_id=1, source_target_pairs={{0,64},{16,80},{32,96},{48,112},{64,0},{80,16},{96,32},{112,48},{1... | collective-permute-start | bytes 196616 | tf_op jit(solution)/shard_map/ppermute | solution.py:415
  51.5 13.6 %collective-permute-start.22 = (s16[1040,128]{1,0:T(8,128)(2,1)S(1)}, s16[1040,128]{1,0:T(8,128)(2,1)S(1)}, u32[]{:S(2)}, u32[]{:S(2)}) collective-permute-start(s16[1040,128]{1,0:T(8,128)(2,1)S(1)} %get-tuple-element.73), channel_id=1, source_target_pairs={{0,4},{1,5},{2,6},{3,7},{4,8},{5,9},{6,10},{7,11},{8,12},{9,13},{1... | collective-permute-start | bytes 798728 | tf_op jit(solution)/shard_map/ppermute | solution.py:378
  55.4 11.0 %collective-permute-start.23 = (s16[1040,128]{1,0:T(8,128)(2,1)S(1)}, s16[1040,128]{1,0:T(8,128)(2,1)S(1)}, u32[]{:S(2)}, u32[]{:S(2)}) collective-permute-start(s16[1040,128]{1,0:T(8,128)(2,1)S(1)} %get-tuple-element.74), channel_id=1, source_target_pairs={{0,8},{1,9},{2,10},{3,11},{4,12},{5,13},{6,14},{7,15},{8,0},{9,1},... | collective-permute-start | bytes 798728 | tf_op jit(solution)/shard_map/ppermute | solution.py:378
  60.2 8.9 %collective-permute-start.24 = (s16[1040,128]{1,0:T(8,128)(2,1)S(1)}, s16[1040,128]{1,0:T(8,128)(2,1)S(1)}, u32[]{:S(2)}, u32[]{:S(2)}) collective-permute-start(s16[1040,128]{1,0:T(8,128)(2,1)S(1)} %get-tuple-element.75), channel_id=1, source_target_pairs={{0,12},{1,13},{2,14},{3,15},{4,0},{5,1},{6,2},{7,3},{8,4},{9,5},{1... | collective-permute-start | bytes 798728 | tf_op jit(solution)/shard_map/ppermute | solution.py:378
  63.0 8.3 %collective-permute-start.28 = (f32[2,64,128]{2,1,0:T(8,128)S(1)}, f32[2,64,128]{2,1,0:T(8,128)S(1)}, u32[]{:S(2)}, u32[]{:S(2)}) collective-permute-start(f32[2,64,128]{2,1,0:T(8,128)S(1)} %folded.12.a_ref), channel_id=1, source_target_pairs={{0,128},{16,144},{32,160},{48,176},{64,192},{80,208},{96,224},{112... | collective-permute-start | bytes 196616 | tf_op jit(solution)/shard_map/ppermute | solution.py:420
  69.7 6.9 %collective-permute-start.25 = (s16[272,128]{1,0:T(8,128)(2,1)S(1)}, s16[272,128]{1,0:T(8,128)(2,1)S(1)}, u32[]{:S(2)}, u32[]{:S(2)}) collective-permute-start(s16[272,128]{1,0:T(8,128)(2,1)S(1)} %get-tuple-element.77), channel_id=1, source_target_pairs={{0,1},{1,2},{2,3},{3,0},{4,5},{5,6},{6,7},{7,4},{8,9},{9,10},{10,1... | collective-permute-start | bytes 208904 | tf_op jit(solution)/shard_map/ppermute | solution.py:378
  71.3 8.0 %collective-permute-start.29 = (f32[64,128]{1,0:T(8,128)S(1)}, f32[64,128]{1,0:T(8,128)S(1)}, u32[]{:S(2)}, u32[]{:S(2)}) collective-permute-start(f32[64,128]{1,0:T(8,128)S(1)} %folded.13.mine_ref), channel_id=1, source_target_pairs={{0,16},{16,0},{32,48},{48,32},{64,80},{80,64},{96,112},{112,96},{1... | collective-permute-start | bytes 98312 | tf_op jit(solution)/shard_map/ppermute | solution.py:424
  71.4 12.5 %collective-permute-start.26 = (s16[272,128]{1,0:T(8,128)(2,1)S(1)}, s16[272,128]{1,0:T(8,128)(2,1)S(1)}, u32[]{:S(2)}, u32[]{:S(2)}) collective-permute-start(s16[272,128]{1,0:T(8,128)(2,1)S(1)} %get-tuple-element.78), channel_id=1, source_target_pairs={{0,2},{1,3},{2,0},{3,1},{4,6},{5,7},{6,4},{7,5},{8,10},{9,11},{10,... | collective-permute-start | bytes 208904 | tf_op jit(solution)/shard_map/ppermute | solution.py:378
  72.5 11.3 %collective-permute-start.27 = (s16[272,128]{1,0:T(8,128)(2,1)S(1)}, s16[272,128]{1,0:T(8,128)(2,1)S(1)}, u32[]{:S(2)}, u32[]{:S(2)}) collective-permute-start(s16[272,128]{1,0:T(8,128)(2,1)S(1)} %get-tuple-element.79), channel_id=1, source_target_pairs={{0,3},{1,0},{2,1},{3,2},{4,7},{5,4},{6,5},{7,6},{8,11},{9,8},{10,9... | collective-permute-start | bytes 208904 | tf_op jit(solution)/shard_map/ppermute | solution.py:378
  75.1 8.7 %collective-permute-start.19 = (s16[272,128]{1,0:T(8,128)(2,1)S(1)}, s16[272,128]{1,0:T(8,128)(2,1)S(1)}, u32[]{:S(2)}, u32[]{:S(2)}) collective-permute-start(s16[272,128]{1,0:T(8,128)(2,1)S(1)} %get-tuple-element.70), channel_id=1, source_target_pairs={{0,4},{1,5},{2,6},{3,7},{4,8},{5,9},{6,10},{7,11},{8,12},{9,13},{1... | collective-permute-start | bytes 208904 | tf_op jit(solution)/shard_map/ppermute | solution.py:378
  76.6 7.3 %collective-permute-start.20 = (s16[272,128]{1,0:T(8,128)(2,1)S(1)}, s16[272,128]{1,0:T(8,128)(2,1)S(1)}, u32[]{:S(2)}, u32[]{:S(2)}) collective-permute-start(s16[272,128]{1,0:T(8,128)(2,1)S(1)} %get-tuple-element.71), channel_id=1, source_target_pairs={{0,8},{1,9},{2,10},{3,11},{4,12},{5,13},{6,14},{7,15},{8,0},{9,1},... | collective-permute-start | bytes 208904 | tf_op jit(solution)/shard_map/ppermute | solution.py:378
  79.2 4.7 %collective-permute-start.21 = (s16[272,128]{1,0:T(8,128)(2,1)S(1)}, s16[272,128]{1,0:T(8,128)(2,1)S(1)}, u32[]{:S(2)}, u32[]{:S(2)}) collective-permute-start(s16[272,128]{1,0:T(8,128)(2,1)S(1)} %get-tuple-element.72), channel_id=1, source_target_pairs={{0,12},{1,13},{2,14},{3,15},{4,0},{5,1},{6,2},{7,3},{8,4},{9,5},{1... | collective-permute-start | bytes 208904 | tf_op jit(solution)/shard_map/ppermute | solution.py:378
  (2 other events, 12.1 us)

commit v3 on v2

--- a/solution.py
+++ b/solution.py
@@ -38,25 +38,34 @@
 def build_body(v_ref, u_ref, after_ref, high_ref, low_ref, acc_ref, *, block):
     del after_ref
     pitch = block + 1
-    hi_iota = lax.broadcasted_iota(jnp.int32, (HI, FIBER), 0)
-    lo_iota = lax.broadcasted_iota(jnp.int32, (LO, FIBER), 0)
+    narrow = jnp.bfloat16
+    hi_iota = lax.broadcasted_iota(jnp.int32, (HI, FIBER), 0).astype(narrow)
+    lo_iota = lax.broadcasted_iota(jnp.int32, (LO, FIBER), 0).astype(narrow)
+    zero = jnp.zeros((HI, FIBER), narrow)
+
+    def spread(row, rows):
+        return jnp.concatenate([jnp.broadcast_to(row, (16, FIBER)).astype(narrow)] * (rows // 16), axis=0)
+
+    def hits(t):
+        v = v_ref[pl.ds(t, 1), :]
+        u = u_ref[pl.ds(t, 1), :]
+        vh = v.astype(narrow).astype(jnp.float32)
+        hit = hi_iota == spread((u >> 7).astype(jnp.float32), HI)
+        low = lo_iota == spread((u & 127).astype(jnp.float32), LO)
+        one = jnp.where(low, jnp.ones((LO, FIBER), narrow), jnp.zeros((LO, FIBER), narrow))
+        return jnp.where(hit, spread(vh, HI), zero), jnp.where(hit, spread(v - vh, HI), zero), one
 
     def add_block(g, carry):
         at = pl.multiple_of(g * block, block)
-        for k in range(block):
-            v = v_ref[pl.ds(at + k, 1), :]
-            u = u_ref[pl.ds(at + k, 1), :]
-            vh = v.astype(jnp.bfloat16).astype(jnp.float32)
-            vl = v - vh
-            hit = hi_iota == (u >> 7)
-            left = jnp.concatenate(
-                [jnp.where(hit, vh, 0.0).astype(jnp.bfloat16), jnp.where(hit, vl, 0.0).astype(jnp.bfloat16)], axis=1
-            )
-            one = jnp.where(lo_iota == (u & 127), 1.0, 0.0).astype(jnp.bfloat16)
-            right = jnp.concatenate([one, one], axis=1)
-            acc_ref[pl.ds(k, HI, stride=pitch), :] = lax.dot_general(
-                left, right, NT, preferred_element_type=jnp.float32
-            )
+        for k in range(0, block, 2):
+            a, a_low, a_one = hits(at + k)
+            b, b_low, b_one = hits(at + k + 1)
+            rows = [(a, zero), (a_low, zero), (zero, b), (zero, b_low)]
+            left = jnp.concatenate([jnp.concatenate(row, axis=1) for row in rows], axis=0)
+            right = jnp.concatenate([a_one, b_one], axis=1)
+            both = lax.dot_general(left, right, NT, preferred_element_type=jnp.float32)
+            acc_ref[pl.ds(k, HI, stride=pitch), :] = both[:HI] + both[HI : 2 * HI]
+            acc_ref[pl.ds(k + 1, HI, stride=pitch), :] = both[2 * HI : 3 * HI] + both[3 * HI :]
         for h in range(HI):
             weight = acc_ref[pl.ds(h * pitch, block), :]
             high = weight.astype(jnp.bfloat16)

time: 85.3 us -> 84.1 us (0.986)
  Pallas kernels: 27.3 us -> 25 us
  starting transfers between devices: 44.1 us -> 46.4 us
  waiting for transfers between devices: 11 us -> 9.56 us
    pallas_call x4, Pallas kernels: 15 us -> 12.7 us  [build_weights(): pl.pallas_call(functools.partial(build_body, block=block), grid=(1,), in_...]
    ppermute x4, starting transfers between devices: 10.8 us -> 9.16 us  [on_device(): lax.ppermute(found[-1] if step < 3 else found[-1][:2 * ROWS], 'rows', aro...]
    ppermute x12, waiting for transfers between devices: 6.87 us -> 5.23 us  [along(): lax.ppermute(xs[k - 1], 'cols', moved(k))]
    ppermute x1, starting transfers between devices: 2.1 us -> 3.26 us  [on_device(): more = lax.ppermute(grams, 'rows', swapped(8))]
    ppermute x4, starting transfers between devices: 1.34 us -> 2.31 us  [on_device(): pieces = found + [lax.ppermute(x, 'rows', across) for x in found[1:]]]
  transfers between devices with their start and end apart: 30 -> 30, of which waited for: 6 -> 9; matrix products, arithmetic and copies ran while one was open for 2% -> 2% of each run, Pallas kernels for 26% -> 24%
where the time goes in v3:
time: 84.1 us; the launch traced here: 83.6 us
  starting transfers between devices  46.4 us (55%)
  Pallas kernels  25 us (30%)
  waiting for transfers between devices  9.56 us (11%)
  local copies, waits for them, and re-layouts  1.75 us (2%)
  between operations  0.94 us (1%)
    ppermute x12, starting transfers between devices, along(): lax.ppermute(xs[k - 1], 'cols', moved(k))  18.9 us
    pallas_call x4, Pallas kernels, build_weights(): pl.pallas_call(functools.partial(build_body, block=block), grid=(1,), in_...  12.7 us
    ppermute x4, starting transfers between devices, on_device(): lax.ppermute(found[-1] if step < 3 else found[-1][:2 * ROWS], 'rows', aro...  9.16 us
    ppermute x3, starting transfers between devices, on_device(): lax.ppermute(grams, *(('cols', swapped(2 << step)) if step < 3 else ('row...  5.96 us
    pallas_call x2, Pallas kernels, products(): pl.pallas_call(functools.partial(product_body, along_x=along_x, sizes=siz...  5.54 us
    ppermute x12, waiting for transfers between devices, along(): lax.ppermute(xs[k - 1], 'cols', moved(k))  5.23 us
    pallas_call x1, Pallas kernels, inverted(): pl.pallas_call(functools.partial(inverse_body, me=me), in_specs=[in_vmem,...  4 us
    ppermute x1, starting transfers between devices, on_device(): more = lax.ppermute(grams, 'rows', swapped(8))  3.26 us
  transfers between devices with their start and end apart: 30, of which 9 were waited for; matrix products, arithmetic and copies ran while one was open for 2% of the time, Pallas kernels for 24%

profile of v3, /device:TPU:32, one launch (start us, length us, event | category | flops | bytes accessed | tf_op | source)
XLA Modules:
  0.0 83.6 jit_solution(14901086828972705787)
XLA Ops:
  2.6 2.0 %collective-permute-start.2 = (bf16[1024,128]{1,0:T(8,128)(2,1)S(1)}, bf16[1024,128]{1,0:T(8,128)(2,1)S(1)}, u32[]{:S(2)}, u32[]{:S(2)}) collective-permute-start(bf16[1024,128]{1,0:T(8,128)(2,1)S(1)} %constant_dynamic-update-slice_fusion.after_ref.refs_0_.refs_3_), channel_id=1, source_target_pairs={{0,32},{32,64},{64,96},{96,128},{128,160},{160,192},{192,224},{224... | collective-permute-start | bytes 786440 | tf_op jit(solution)/shard_map/ppermute | solution.py:401
  4.5 1.5 %collective-permute-start.3 = (f32[2,64,128]{2,1,0:T(8,128)S(1)}, f32[2,64,128]{2,1,0:T(8,128)S(1)}, u32[]{:S(2)}, u32[]{:S(2)}) collective-permute-start(f32[2,64,128]{2,1,0:T(8,128)S(1)} %partial_grams.1.a_ref), channel_id=1, source_target_pairs={{0,1},{1,0},{2,3},{3,2},{4,5},{5,4},{6,7},{7,6},{8,9},{9,8},{10,11... | collective-permute-start | bytes 196616 | tf_op jit(solution)/shard_map/ppermute | solution.py:399
  6.0 3.3 %build_weights.4 = (bf16[64,128,128]{2,1,0:T(8,128)(2,1)S(1)}, bf16[64,128,128]{2,1,0:T(8,128)(2,1)S(1)}) custom-call(f32[512,128]{1,0:T(8,128)S(1)} %copy-done.2, s32[512,128]{1,0:T(8,128)S(1)} %copy-done.3, bf16[1024,128]{1,0:T(8,128)(2,1)S(1)} %constant_dynamic-update-slice_fusion.after_ref.refs_0_.refs_3_), custom_call_target="tpu_custom_call" | custom-call | flops 6000000000 | bytes 20000000 | tf_op jit(solution)/shard_map/build_weights/pallas_call | solution.py:80
  9.4 2.8 %collective-permute-start.6 = (f32[2,64,128]{2,1,0:T(8,128)S(1)}, f32[2,64,128]{2,1,0:T(8,128)S(1)}, u32[]{:S(2)}, u32[]{:S(2)}) collective-permute-start(f32[2,64,128]{2,1,0:T(8,128)S(1)} %folded.7.a_ref), channel_id=1, source_target_pairs={{0,2},{1,3},{2,0},{3,1},{4,6},{5,7},{6,4},{7,5},{8,10},{9,11},{10,... | collective-permute-start | bytes 196616 | tf_op jit(solution)/shard_map/ppermute | solution.py:406
  12.2 1.9 %collective-permute-start.4 = (bf16[1024,128]{1,0:T(8,128)(2,1)S(1)}, bf16[1024,128]{1,0:T(8,128)(2,1)S(1)}, u32[]{:S(2)}, u32[]{:S(2)}) collective-permute-start(bf16[1024,128]{1,0:T(8,128)(2,1)S(1)} %collective-permute-done.2.after_ref.refs_4_), channel_id=1, source_target_pairs={{0,32},{32,64},{64,96},{96,128},{128,160},{160,192},{192,224},{224... | collective-permute-start | bytes 786440 | tf_op jit(solution)/shard_map/ppermute | solution.py:401
  14.1 3.1 %build_weights.5 = (bf16[64,128,128]{2,1,0:T(8,128)(2,1)S(1)}, bf16[64,128,128]{2,1,0:T(8,128)(2,1)S(1)}) custom-call(f32[512,128]{1,0:T(8,128)S(1)} %copy-done.2, s32[512,128]{1,0:T(8,128)S(1)} %copy-done.3, bf16[1024,128]{1,0:T(8,128)(2,1)S(1)} %collective-permute-done.2.after_ref.refs_4_), custom_call_target="tpu_custom_call" | custom-call | flops 6000000000 | bytes 20000000 | tf_op jit(solution)/shard_map/build_weights/pallas_call | solution.py:80
  17.2 1.7 %collective-permute-start.7 = (f32[2,64,128]{2,1,0:T(8,128)S(1)}, f32[2,64,128]{2,1,0:T(8,128)S(1)}, u32[]{:S(2)}, u32[]{:S(2)}) collective-permute-start(f32[2,64,128]{2,1,0:T(8,128)S(1)} %folded.8.a_ref), channel_id=1, source_target_pairs={{0,4},{1,5},{2,6},{3,7},{4,0},{5,1},{6,2},{7,3},{8,12},{9,13},{10,... | collective-permute-start | bytes 196616 | tf_op jit(solution)/shard_map/ppermute | solution.py:409
  20.3 2.2 %collective-permute-start.5 = (bf16[1024,128]{1,0:T(8,128)(2,1)S(1)}, bf16[1024,128]{1,0:T(8,128)(2,1)S(1)}, u32[]{:S(2)}, u32[]{:S(2)}) collective-permute-start(bf16[1024,128]{1,0:T(8,128)(2,1)S(1)} %collective-permute-done.4.after_ref.refs_5_), channel_id=1, source_target_pairs={{0,32},{32,64},{64,96},{96,128},{128,160},{160,192},{192,224},{224... | collective-permute-start | bytes 786440 | tf_op jit(solution)/shard_map/ppermute | solution.py:401
  22.5 3.0 %collective-permute-start.8 = (f32[2,64,128]{2,1,0:T(8,128)S(1)}, f32[2,64,128]{2,1,0:T(8,128)S(1)}, u32[]{:S(2)}, u32[]{:S(2)}) collective-permute-start(f32[2,64,128]{2,1,0:T(8,128)S(1)} %folded.9.a_ref), channel_id=1, source_target_pairs={{0,8},{1,9},{2,10},{3,11},{4,12},{5,13},{6,14},{7,15},{8,0},{9,1},... | collective-permute-start | bytes 196616 | tf_op jit(solution)/shard_map/ppermute | solution.py:409
  25.5 3.1 %build_weights.6 = (bf16[64,128,128]{2,1,0:T(8,128)(2,1)S(1)}, bf16[64,128,128]{2,1,0:T(8,128)(2,1)S(1)}) custom-call(f32[512,128]{1,0:T(8,128)S(1)} %copy-done.2, s32[512,128]{1,0:T(8,128)S(1)} %copy-done.3, bf16[1024,128]{1,0:T(8,128)(2,1)S(1)} %collective-permute-done.4.after_ref.refs_5_), custom_call_target="tpu_custom_call" | custom-call | flops 6000000000 | bytes 20000000 | tf_op jit(solution)/shard_map/build_weights/pallas_call | solution.py:80
  28.8 1.2 %collective-permute-start.13 = (bf16[1024,128]{1,0:T(8,128)(2,1)S(1)}, bf16[1024,128]{1,0:T(8,128)(2,1)S(1)}, u32[]{:S(2)}, u32[]{:S(2)}) collective-permute-start(bf16[1024,128]{1,0:T(8,128)(2,1)S(1)} %collective-permute-done.5.after_ref.refs_6_), channel_id=1, source_target_pairs={{0,16},{16,0},{32,48},{48,32},{64,80},{80,64},{96,112},{112,96},{1... | collective-permute-start | bytes 786440 | tf_op jit(solution)/shard_map/ppermute | solution.py:417
  30.1 1.3 %collective-permute-start.10 = (f32[2,64,128]{2,1,0:T(8,128)S(1)}, f32[2,64,128]{2,1,0:T(8,128)S(1)}, u32[]{:S(2)}, u32[]{:S(2)}) collective-permute-start(f32[2,64,128]{2,1,0:T(8,128)S(1)} %folded.10.a_ref), channel_id=1, source_target_pairs={{0,32},{16,48},{32,0},{48,16},{64,96},{80,112},{96,64},{112,80},{1... | collective-permute-start | bytes 196616 | tf_op jit(solution)/shard_map/ppermute | solution.py:409
  31.4 3.1 %collective-permute-start.9 = (bf16[512,128]{1,0:T(8,128)(2,1)S(1)}, bf16[512,128]{1,0:T(8,128)(2,1)S(1)}, u32[]{:S(2)}, u32[]{:S(2)}) collective-permute-start(bf16[512,128]{1,0:T(8,128)(2,1)S(1)} %slice.3), channel_id=1, source_target_pairs={{0,32},{32,64},{64,96},{96,128},{128,160},{160,192},{192,224},{224... | collective-permute-start | bytes 393224 | tf_op jit(solution)/shard_map/ppermute | solution.py:401
  34.4 3.3 %build_weights.7 = (bf16[64,128,128]{2,1,0:T(8,128)(2,1)S(1)}, bf16[64,128,128]{2,1,0:T(8,128)(2,1)S(1)}) custom-call(f32[512,128]{1,0:T(8,128)S(1)} %copy-done.2, s32[512,128]{1,0:T(8,128)S(1)} %copy-done.3, bf16[1024,128]{1,0:T(8,128)(2,1)S(1)} %collective-permute-done.5.after_ref.refs_6_), custom_call_target="tpu_custom_call" | custom-call | flops 6000000000 | bytes 20000000 | tf_op jit(solution)/shard_map/build_weights/pallas_call | solution.py:80
  39.4 3.7 %products.2 = (s16[1040,128]{1,0:T(8,128)(2,1)S(1)}, s16[1040,128]{1,0:T(8,128)(2,1)S(1)}, s16[1040,128]{1,0:T(8,128)(2,1)S(1)}, f32[4,128,256]{2,1,0:T(8,128)S(1)}, bf16[256,512]{1,0:T(8,128)(2,1)S(1)}) custom-call(s32[512]{0:T(512)S(1)} %copy-done, s32[512]{0:T(512)S(1)} %copy-done.1, s32[1]{0:T(128)S(6)} %copy.11.refs_2_, ...), custom_call_target="tpu_custom_call" | custom-call | flops 4000000000 | bytes 13000000 | tf_op jit(solution)/shard_map/products/pallas_call | solution.py:205
  43.8 2.0 %collective-permute-start.17 = (s16[1040,128]{1,0:T(8,128)(2,1)S(1)}, s16[1040,128]{1,0:T(8,128)(2,1)S(1)}, u32[]{:S(2)}, u32[]{:S(2)}) collective-permute-start(s16[1040,128]{1,0:T(8,128)(2,1)S(1)} %get-tuple-element.67), channel_id=1, source_target_pairs={{0,2},{1,3},{2,0},{3,1},{4,6},{5,7},{6,4},{7,5},{8,10},{9,11},{10,... | collective-permute-start | bytes 798728 | tf_op jit(solution)/shard_map/ppermute | solution.py:387
  46.5 1.9 %products.3 = (s16[1040,128]{1,0:T(8,128)(2,1)S(1)}, s16[1040,128]{1,0:T(8,128)(2,1)S(1)}, s16[1040,128]{1,0:T(8,128)(2,1)S(1)}, f32[4,128,256]{2,1,0:T(8,128)S(1)}) custom-call(bf16[256,512]{1,0:T(8,128)(2,1)S(1)} %get-tuple-element.62.refs_0_, bf16[64,128,128]{2,1,0:T(8,128)(2,1)S(1)} %get-tuple-element.53.refs_12_.refs_1_, ...), custom_call_target="tpu_custom_call" | custom-call | flops 4000000000 | bytes 13000000 | tf_op jit(solution)/shard_map/products/pallas_call | solution.py:205
  48.4 1.9 %collective-permute-start.15 = (f32[2,64,128]{2,1,0:T(8,128)S(1)}, f32[2,64,128]{2,1,0:T(8,128)S(1)}, u32[]{:S(2)}, u32[]{:S(2)}) collective-permute-start(f32[2,64,128]{2,1,0:T(8,128)S(1)} %folded.11.a_ref), channel_id=1, source_target_pairs={{0,64},{16,80},{32,96},{48,112},{64,0},{80,16},{96,32},{112,48},{1... | collective-permute-start | bytes 196616 | tf_op jit(solution)/shard_map/ppermute | solution.py:424
  50.3 1.0 %collective-permute-start.22 = (s16[1040,128]{1,0:T(8,128)(2,1)S(1)}, s16[1040,128]{1,0:T(8,128)(2,1)S(1)}, u32[]{:S(2)}, u32[]{:S(2)}) collective-permute-start(s16[1040,128]{1,0:T(8,128)(2,1)S(1)} %get-tuple-element.73), channel_id=1, source_target_pairs={{0,4},{1,5},{2,6},{3,7},{4,8},{5,9},{6,10},{7,11},{8,12},{9,13},{1... | collective-permute-start | bytes 798728 | tf_op jit(solution)/shard_map/ppermute | solution.py:387
  51.3 2.4 %collective-permute-done.15.b_ref = f32[2,64,128]{2,1,0:T(8,128)S(1)} collective-permute-done((f32[2,64,128]{2,1,0:T(8,128)S(1)}, f32[2,64,128]{2,1,0:T(8,128)S(1)}, u32[]{:S(2)}, u32[]{:S(2)}) %collective-permute-start.15) | collective-permute-done | bytes 65568 | tf_op jit(solution)/shard_map/ppermute | solution.py:424
  53.7 2.6 %collective-permute-start.23 = (s16[1040,128]{1,0:T(8,128)(2,1)S(1)}, s16[1040,128]{1,0:T(8,128)(2,1)S(1)}, u32[]{:S(2)}, u32[]{:S(2)}) collective-permute-start(s16[1040,128]{1,0:T(8,128)(2,1)S(1)} %get-tuple-element.74), channel_id=1, source_target_pairs={{0,8},{1,9},{2,10},{3,11},{4,12},{5,13},{6,14},{7,15},{8,0},{9,1},... | collective-permute-start | bytes 798728 | tf_op jit(solution)/shard_map/ppermute | solution.py:387
  56.3 2.2 %collective-permute-done.16.a_ref = s16[1040,128]{1,0:T(8,128)(2,1)S(1)} collective-permute-done((s16[1040,128]{1,0:T(8,128)(2,1)S(1)}, s16[1040,128]{1,0:T(8,128)(2,1)S(1)}, u32[]{:S(2)}, u32[]{:S(2)}) %collective-permute-start.16) | collective-permute-done | bytes 266272 | tf_op jit(solution)/shard_map/ppermute | solution.py:387
  58.5 2.7 %collective-permute-start.24 = (s16[1040,128]{1,0:T(8,128)(2,1)S(1)}, s16[1040,128]{1,0:T(8,128)(2,1)S(1)}, u32[]{:S(2)}, u32[]{:S(2)}) collective-permute-start(s16[1040,128]{1,0:T(8,128)(2,1)S(1)} %get-tuple-element.75), channel_id=1, source_target_pairs={{0,12},{1,13},{2,14},{3,15},{4,0},{5,1},{6,2},{7,3},{8,4},{9,5},{1... | collective-permute-start | bytes 798728 | tf_op jit(solution)/shard_map/ppermute | solution.py:387
  61.8 3.3 %collective-permute-start.28 = (f32[2,64,128]{2,1,0:T(8,128)S(1)}, f32[2,64,128]{2,1,0:T(8,128)S(1)}, u32[]{:S(2)}, u32[]{:S(2)}) collective-permute-start(f32[2,64,128]{2,1,0:T(8,128)S(1)} %folded.12.a_ref), channel_id=1, source_target_pairs={{0,128},{16,144},{32,160},{48,176},{64,192},{80,208},{96,224},{112... | collective-permute-start | bytes 196616 | tf_op jit(solution)/shard_map/ppermute | solution.py:429
  65.7 2.3 %collective-permute-done.24.c_ref = s16[1040,128]{1,0:T(8,128)(2,1)S(1)} collective-permute-done((s16[1040,128]{1,0:T(8,128)(2,1)S(1)}, s16[1040,128]{1,0:T(8,128)(2,1)S(1)}, u32[]{:S(2)}, u32[]{:S(2)}) %collective-permute-start.24) | collective-permute-done | bytes 266272 | tf_op jit(solution)/shard_map/ppermute | solution.py:387
  68.6 1.0 %collective-permute-start.25 = (s16[272,128]{1,0:T(8,128)(2,1)S(1)}, s16[272,128]{1,0:T(8,128)(2,1)S(1)}, u32[]{:S(2)}, u32[]{:S(2)}) collective-permute-start(s16[272,128]{1,0:T(8,128)(2,1)S(1)} %get-tuple-element.77), channel_id=1, source_target_pairs={{0,1},{1,2},{2,3},{3,0},{4,5},{5,6},{6,7},{7,4},{8,9},{9,10},{10,1... | collective-permute-start | bytes 208904 | tf_op jit(solution)/shard_map/ppermute | solution.py:387
  70.2 1.2 %collective-permute-start.26 = (s16[272,128]{1,0:T(8,128)(2,1)S(1)}, s16[272,128]{1,0:T(8,128)(2,1)S(1)}, u32[]{:S(2)}, u32[]{:S(2)}) collective-permute-start(s16[272,128]{1,0:T(8,128)(2,1)S(1)} %get-tuple-element.78), channel_id=1, source_target_pairs={{0,2},{1,3},{2,0},{3,1},{4,6},{5,7},{6,4},{7,5},{8,10},{9,11},{10,... | collective-permute-start | bytes 208904 | tf_op jit(solution)/shard_map/ppermute | solution.py:387
  71.4 2.6 %collective-permute-start.27 = (s16[272,128]{1,0:T(8,128)(2,1)S(1)}, s16[272,128]{1,0:T(8,128)(2,1)S(1)}, u32[]{:S(2)}, u32[]{:S(2)}) collective-permute-start(s16[272,128]{1,0:T(8,128)(2,1)S(1)} %get-tuple-element.79), channel_id=1, source_target_pairs={{0,3},{1,0},{2,1},{3,2},{4,7},{5,4},{6,5},{7,6},{8,11},{9,8},{10,9... | collective-permute-start | bytes 208904 | tf_op jit(solution)/shard_map/ppermute | solution.py:387
  74.0 1.0 %collective-permute-start.19 = (s16[272,128]{1,0:T(8,128)(2,1)S(1)}, s16[272,128]{1,0:T(8,128)(2,1)S(1)}, u32[]{:S(2)}, u32[]{:S(2)}) collective-permute-start(s16[272,128]{1,0:T(8,128)(2,1)S(1)} %get-tuple-element.70), channel_id=1, source_target_pairs={{0,4},{1,5},{2,6},{3,7},{4,8},{5,9},{6,10},{7,11},{8,12},{9,13},{1... | collective-permute-start | bytes 208904 | tf_op jit(solution)/shard_map/ppermute | solution.py:387
  74.9 3.1 %collective-permute-start.20 = (s16[272,128]{1,0:T(8,128)(2,1)S(1)}, s16[272,128]{1,0:T(8,128)(2,1)S(1)}, u32[]{:S(2)}, u32[]{:S(2)}) collective-permute-start(s16[272,128]{1,0:T(8,128)(2,1)S(1)} %get-tuple-element.71), channel_id=1, source_target_pairs={{0,8},{1,9},{2,10},{3,11},{4,12},{5,13},{6,14},{7,15},{8,0},{9,1},... | collective-permute-start | bytes 208904 | tf_op jit(solution)/shard_map/ppermute | solution.py:387
  78.2 4.0 %inverted.1.refs_8_ = f32[128,128]{1,0:T(8,128)S(1)} custom-call(f32[64,128]{1,0:T(8,128)S(1)} %folded.13.mine_ref, f32[64,128]{1,0:T(8,128)S(1)} %collective-permute-done.29.other_ref), custom_call_target="tpu_custom_call" | custom-call | flops 4000000000 | bytes 15000000 | tf_op jit(solution)/shard_map/inverted/pallas_call | solution.py:365
  82.4 1.3 %finish.1 = f32[512,128]{1,0:T(8,128)} custom-call(f32[128,256]{1,0:T(8,128)S(1)} %get-tuple-element.69.after_ref.refs_0_, s16[272,128]{1,0:T(8,128)(2,1)S(1)} %collective-permute-done.19.refs_1_, s16[272,128]{1,0:T(8,128)(2,1)S(1)} %collective-permute-done.20.refs_2_, s16[272,128]{1,0:T(8,128)(2,1)S(1)} %collective-permute-done.21.refs_3_, ...), custom_call_target="tpu_custom_call" | custom-call | tf_op jit(solution)/shard_map/finish/pallas_call | solution.py:273
  (59 shorter events, 9.3 us)
Async XLA Ops:
  0.0 2.2 %collective-permute-start = (bf16[256,128]{1,0:T(8,128)(2,1)}, bf16[256,128]{1,0:T(8,128)(2,1)S(1)}, u32[]{:S(2)}, u32[]{:S(2)}) collective-permute-start(bf16[256,128]{1,0:T(8,128)(2,1)} %param.12), channel_id=1, source_target_pairs={{0,16},{16,0},{32,48},{48,32},{64,80},{80,64},{96,112},{112,96},{1... | collective-permute-start | bytes 196616 | tf_op jit(solution)/shard_map/ppermute | solution.py:395
  0.0 2.2 %collective-permute-start.1 = (bf16[256,128]{1,0:T(8,128)(2,1)}, bf16[256,128]{1,0:T(8,128)(2,1)S(1)}, u32[]{:S(2)}, u32[]{:S(2)}) collective-permute-start(bf16[256,128]{1,0:T(8,128)(2,1)} %param.13), channel_id=1, source_target_pairs={{0,16},{16,0},{32,48},{48,32},{64,80},{80,64},{96,112},{112,96},{1... | collective-permute-start | bytes 196616 | tf_op jit(solution)/shard_map/ppermute | solution.py:395
  2.6 6.8 %collective-permute-start.2 = (bf16[1024,128]{1,0:T(8,128)(2,1)S(1)}, bf16[1024,128]{1,0:T(8,128)(2,1)S(1)}, u32[]{:S(2)}, u32[]{:S(2)}) collective-permute-start(bf16[1024,128]{1,0:T(8,128)(2,1)S(1)} %constant_dynamic-update-slice_fusion.after_ref.refs_0_.refs_3_), channel_id=1, source_target_pairs={{0,32},{32,64},{64,96},{96,128},{128,160},{160,192},{192,224},{224... | collective-permute-start | bytes 786440 | tf_op jit(solution)/shard_map/ppermute | solution.py:401
  4.5 4.8 %collective-permute-start.3 = (f32[2,64,128]{2,1,0:T(8,128)S(1)}, f32[2,64,128]{2,1,0:T(8,128)S(1)}, u32[]{:S(2)}, u32[]{:S(2)}) collective-permute-start(f32[2,64,128]{2,1,0:T(8,128)S(1)} %partial_grams.1.a_ref), channel_id=1, source_target_pairs={{0,1},{1,0},{2,3},{3,2},{4,5},{5,4},{6,7},{7,6},{8,9},{9,8},{10,11... | collective-permute-start | bytes 196616 | tf_op jit(solution)/shard_map/ppermute | solution.py:399
  9.4 7.8 %collective-permute-start.6 = (f32[2,64,128]{2,1,0:T(8,128)S(1)}, f32[2,64,128]{2,1,0:T(8,128)S(1)}, u32[]{:S(2)}, u32[]{:S(2)}) collective-permute-start(f32[2,64,128]{2,1,0:T(8,128)S(1)} %folded.7.a_ref), channel_id=1, source_target_pairs={{0,2},{1,3},{2,0},{3,1},{4,6},{5,7},{6,4},{7,5},{8,10},{9,11},{10,... | collective-permute-start | bytes 196616 | tf_op jit(solution)/shard_map/ppermute | solution.py:406
  12.2 8.1 %collective-permute-start.4 = (bf16[1024,128]{1,0:T(8,128)(2,1)S(1)}, bf16[1024,128]{1,0:T(8,128)(2,1)S(1)}, u32[]{:S(2)}, u32[]{:S(2)}) collective-permute-start(bf16[1024,128]{1,0:T(8,128)(2,1)S(1)} %collective-permute-done.2.after_ref.refs_4_), channel_id=1, source_target_pairs={{0,32},{32,64},{64,96},{96,128},{128,160},{160,192},{192,224},{224... | collective-permute-start | bytes 786440 | tf_op jit(solution)/shard_map/ppermute | solution.py:401
  17.2 5.3 %collective-permute-start.7 = (f32[2,64,128]{2,1,0:T(8,128)S(1)}, f32[2,64,128]{2,1,0:T(8,128)S(1)}, u32[]{:S(2)}, u32[]{:S(2)}) collective-permute-start(f32[2,64,128]{2,1,0:T(8,128)S(1)} %folded.8.a_ref), channel_id=1, source_target_pairs={{0,4},{1,5},{2,6},{3,7},{4,0},{5,1},{6,2},{7,3},{8,12},{9,13},{10,... | collective-permute-start | bytes 196616 | tf_op jit(solution)/shard_map/ppermute | solution.py:409
  18.9 19.8 %collective-permute-start.11 = (bf16[1024,128]{1,0:T(8,128)(2,1)S(1)}, bf16[1024,128]{1,0:T(8,128)(2,1)S(1)}, u32[]{:S(2)}, u32[]{:S(2)}) collective-permute-start(bf16[1024,128]{1,0:T(8,128)(2,1)S(1)} %collective-permute-done.2.after_ref.refs_4_), channel_id=1, source_target_pairs={{0,16},{16,0},{32,48},{48,32},{64,80},{80,64},{96,112},{112,96},{1... | collective-permute-start | bytes 786440 | tf_op jit(solution)/shard_map/ppermute | solution.py:417
  20.3 18.4 %collective-permute-start.12 = (bf16[1024,128]{1,0:T(8,128)(2,1)S(1)}, bf16[1024,128]{1,0:T(8,128)(2,1)S(1)}, u32[]{:S(2)}, u32[]{:S(2)}) collective-permute-start(bf16[1024,128]{1,0:T(8,128)(2,1)S(1)} %collective-permute-done.4.after_ref.refs_5_), channel_id=1, source_target_pairs={{0,16},{16,0},{32,48},{48,32},{64,80},{80,64},{96,112},{112,96},{1... | collective-permute-start | bytes 786440 | tf_op jit(solution)/shard_map/ppermute | solution.py:417
  20.3 8.5 %collective-permute-start.5 = (bf16[1024,128]{1,0:T(8,128)(2,1)S(1)}, bf16[1024,128]{1,0:T(8,128)(2,1)S(1)}, u32[]{:S(2)}, u32[]{:S(2)}) collective-permute-start(bf16[1024,128]{1,0:T(8,128)(2,1)S(1)} %collective-permute-done.4.after_ref.refs_5_), channel_id=1, source_target_pairs={{0,32},{32,64},{64,96},{96,128},{128,160},{160,192},{192,224},{224... | collective-permute-start | bytes 786440 | tf_op jit(solution)/shard_map/ppermute | solution.py:401
  22.5 6.3 %collective-permute-start.8 = (f32[2,64,128]{2,1,0:T(8,128)S(1)}, f32[2,64,128]{2,1,0:T(8,128)S(1)}, u32[]{:S(2)}, u32[]{:S(2)}) collective-permute-start(f32[2,64,128]{2,1,0:T(8,128)S(1)} %folded.9.a_ref), channel_id=1, source_target_pairs={{0,8},{1,9},{2,10},{3,11},{4,12},{5,13},{6,14},{7,15},{8,0},{9,1},... | collective-permute-start | bytes 196616 | tf_op jit(solution)/shard_map/ppermute | solution.py:409
  28.8 10.6 %collective-permute-start.13 = (bf16[1024,128]{1,0:T(8,128)(2,1)S(1)}, bf16[1024,128]{1,0:T(8,128)(2,1)S(1)}, u32[]{:S(2)}, u32[]{:S(2)}) collective-permute-start(bf16[1024,128]{1,0:T(8,128)(2,1)S(1)} %collective-permute-done.5.after_ref.refs_6_), channel_id=1, source_target_pairs={{0,16},{16,0},{32,48},{48,32},{64,80},{80,64},{96,112},{112,96},{1... | collective-permute-start | bytes 786440 | tf_op jit(solution)/shard_map/ppermute | solution.py:417
  30.1 9.3 %copy-start = (s32[512]{0:T(512)S(1)}, s32[512]{0:T(512)}, u32[]{:S(2)}) copy-start(s32[512]{0:T(512)} %refs_0_.1) | copy-start | bytes 6148
  30.1 9.3 %copy-start.1 = (s32[512]{0:T(512)S(1)}, s32[512]{0:T(512)}, u32[]{:S(2)}) copy-start(s32[512]{0:T(512)} %refs_1_.1) | copy-start | bytes 6148
  30.1 7.7 %collective-permute-start.10 = (f32[2,64,128]{2,1,0:T(8,128)S(1)}, f32[2,64,128]{2,1,0:T(8,128)S(1)}, u32[]{:S(2)}, u32[]{:S(2)}) collective-permute-start(f32[2,64,128]{2,1,0:T(8,128)S(1)} %folded.10.a_ref), channel_id=1, source_target_pairs={{0,32},{16,48},{32,0},{48,16},{64,96},{80,112},{96,64},{112,80},{1... | collective-permute-start | bytes 196616 | tf_op jit(solution)/shard_map/ppermute | solution.py:409
  31.4 6.4 %collective-permute-start.9 = (bf16[512,128]{1,0:T(8,128)(2,1)S(1)}, bf16[512,128]{1,0:T(8,128)(2,1)S(1)}, u32[]{:S(2)}, u32[]{:S(2)}) collective-permute-start(bf16[512,128]{1,0:T(8,128)(2,1)S(1)} %slice.3), channel_id=1, source_target_pairs={{0,32},{32,64},{64,96},{96,128},{128,160},{160,192},{192,224},{224... | collective-permute-start | bytes 393224 | tf_op jit(solution)/shard_map/ppermute | solution.py:401
  37.8 1.6 %collective-permute-start.14 = (bf16[512,128]{1,0:T(8,128)(2,1)S(1)}, bf16[512,128]{1,0:T(8,128)(2,1)S(1)}, u32[]{:S(2)}, u32[]{:S(2)}) collective-permute-start(bf16[512,128]{1,0:T(8,128)(2,1)S(1)} %collective-permute-done.9.refs_7_), channel_id=1, source_target_pairs={{0,16},{16,0},{32,48},{48,32},{64,80},{80,64},{96,112},{112,96},{1... | collective-permute-start | bytes 393224 | tf_op jit(solution)/shard_map/ppermute | solution.py:417
  43.1 15.4 %collective-permute-start.16 = (s16[1040,128]{1,0:T(8,128)(2,1)S(1)}, s16[1040,128]{1,0:T(8,128)(2,1)S(1)}, u32[]{:S(2)}, u32[]{:S(2)}) collective-permute-start(s16[1040,128]{1,0:T(8,128)(2,1)S(1)} %get-tuple-element.66), channel_id=1, source_target_pairs={{0,1},{1,2},{2,3},{3,0},{4,5},{5,6},{6,7},{7,4},{8,9},{9,10},{10,1... | collective-permute-start | bytes 798728 | tf_op jit(solution)/shard_map/ppermute | solution.py:387
  43.8 17.5 %collective-permute-start.17 = (s16[1040,128]{1,0:T(8,128)(2,1)S(1)}, s16[1040,128]{1,0:T(8,128)(2,1)S(1)}, u32[]{:S(2)}, u32[]{:S(2)}) collective-permute-start(s16[1040,128]{1,0:T(8,128)(2,1)S(1)} %get-tuple-element.67), channel_id=1, source_target_pairs={{0,2},{1,3},{2,0},{3,1},{4,6},{5,7},{6,4},{7,5},{8,10},{9,11},{10,... | collective-permute-start | bytes 798728 | tf_op jit(solution)/shard_map/ppermute | solution.py:387
  45.7 15.5 %collective-permute-start.18 = (s16[1040,128]{1,0:T(8,128)(2,1)S(1)}, s16[1040,128]{1,0:T(8,128)(2,1)S(1)}, u32[]{:S(2)}, u32[]{:S(2)}) collective-permute-start(s16[1040,128]{1,0:T(8,128)(2,1)S(1)} %get-tuple-element.68), channel_id=1, source_target_pairs={{0,3},{1,0},{2,1},{3,2},{4,7},{5,4},{6,5},{7,6},{8,11},{9,8},{10,9... | collective-permute-start | bytes 798728 | tf_op jit(solution)/shard_map/ppermute | solution.py:387
  48.4 5.3 %collective-permute-start.15 = (f32[2,64,128]{2,1,0:T(8,128)S(1)}, f32[2,64,128]{2,1,0:T(8,128)S(1)}, u32[]{:S(2)}, u32[]{:S(2)}) collective-permute-start(f32[2,64,128]{2,1,0:T(8,128)S(1)} %folded.11.a_ref), channel_id=1, source_target_pairs={{0,64},{16,80},{32,96},{48,112},{64,0},{80,16},{96,32},{112,48},{1... | collective-permute-start | bytes 196616 | tf_op jit(solution)/shard_map/ppermute | solution.py:424
  50.3 14.8 %collective-permute-start.22 = (s16[1040,128]{1,0:T(8,128)(2,1)S(1)}, s16[1040,128]{1,0:T(8,128)(2,1)S(1)}, u32[]{:S(2)}, u32[]{:S(2)}) collective-permute-start(s16[1040,128]{1,0:T(8,128)(2,1)S(1)} %get-tuple-element.73), channel_id=1, source_target_pairs={{0,4},{1,5},{2,6},{3,7},{4,8},{5,9},{6,10},{7,11},{8,12},{9,13},{1... | collective-permute-start | bytes 798728 | tf_op jit(solution)/shard_map/ppermute | solution.py:387
  53.7 12.0 %collective-permute-start.23 = (s16[1040,128]{1,0:T(8,128)(2,1)S(1)}, s16[1040,128]{1,0:T(8,128)(2,1)S(1)}, u32[]{:S(2)}, u32[]{:S(2)}) collective-permute-start(s16[1040,128]{1,0:T(8,128)(2,1)S(1)} %get-tuple-element.74), channel_id=1, source_target_pairs={{0,8},{1,9},{2,10},{3,11},{4,12},{5,13},{6,14},{7,15},{8,0},{9,1},... | collective-permute-start | bytes 798728 | tf_op jit(solution)/shard_map/ppermute | solution.py:387
  58.5 9.5 %collective-permute-start.24 = (s16[1040,128]{1,0:T(8,128)(2,1)S(1)}, s16[1040,128]{1,0:T(8,128)(2,1)S(1)}, u32[]{:S(2)}, u32[]{:S(2)}) collective-permute-start(s16[1040,128]{1,0:T(8,128)(2,1)S(1)} %get-tuple-element.75), channel_id=1, source_target_pairs={{0,12},{1,13},{2,14},{3,15},{4,0},{5,1},{6,2},{7,3},{8,4},{9,5},{1... | collective-permute-start | bytes 798728 | tf_op jit(solution)/shard_map/ppermute | solution.py:387
  61.8 8.3 %collective-permute-start.28 = (f32[2,64,128]{2,1,0:T(8,128)S(1)}, f32[2,64,128]{2,1,0:T(8,128)S(1)}, u32[]{:S(2)}, u32[]{:S(2)}) collective-permute-start(f32[2,64,128]{2,1,0:T(8,128)S(1)} %folded.12.a_ref), channel_id=1, source_target_pairs={{0,128},{16,144},{32,160},{48,176},{64,192},{80,208},{96,224},{112... | collective-permute-start | bytes 196616 | tf_op jit(solution)/shard_map/ppermute | solution.py:429
  68.6 6.4 %collective-permute-start.25 = (s16[272,128]{1,0:T(8,128)(2,1)S(1)}, s16[272,128]{1,0:T(8,128)(2,1)S(1)}, u32[]{:S(2)}, u32[]{:S(2)}) collective-permute-start(s16[272,128]{1,0:T(8,128)(2,1)S(1)} %get-tuple-element.77), channel_id=1, source_target_pairs={{0,1},{1,2},{2,3},{3,0},{4,5},{5,6},{6,7},{7,4},{8,9},{9,10},{10,1... | collective-permute-start | bytes 208904 | tf_op jit(solution)/shard_map/ppermute | solution.py:387
  70.1 8.0 %collective-permute-start.29 = (f32[64,128]{1,0:T(8,128)S(1)}, f32[64,128]{1,0:T(8,128)S(1)}, u32[]{:S(2)}, u32[]{:S(2)}) collective-permute-start(f32[64,128]{1,0:T(8,128)S(1)} %folded.13.mine_ref), channel_id=1, source_target_pairs={{0,16},{16,0},{32,48},{48,32},{64,80},{80,64},{96,112},{112,96},{1... | collective-permute-start | bytes 98312 | tf_op jit(solution)/shard_map/ppermute | solution.py:433
  70.2 12.0 %collective-permute-start.26 = (s16[272,128]{1,0:T(8,128)(2,1)S(1)}, s16[272,128]{1,0:T(8,128)(2,1)S(1)}, u32[]{:S(2)}, u32[]{:S(2)}) collective-permute-start(s16[272,128]{1,0:T(8,128)(2,1)S(1)} %get-tuple-element.78), channel_id=1, source_target_pairs={{0,2},{1,3},{2,0},{3,1},{4,6},{5,7},{6,4},{7,5},{8,10},{9,11},{10,... | collective-permute-start | bytes 208904 | tf_op jit(solution)/shard_map/ppermute | solution.py:387
  71.4 10.9 %collective-permute-start.27 = (s16[272,128]{1,0:T(8,128)(2,1)S(1)}, s16[272,128]{1,0:T(8,128)(2,1)S(1)}, u32[]{:S(2)}, u32[]{:S(2)}) collective-permute-start(s16[272,128]{1,0:T(8,128)(2,1)S(1)} %get-tuple-element.79), channel_id=1, source_target_pairs={{0,3},{1,0},{2,1},{3,2},{4,7},{5,4},{6,5},{7,6},{8,11},{9,8},{10,9... | collective-permute-start | bytes 208904 | tf_op jit(solution)/shard_map/ppermute | solution.py:387
  74.0 8.3 %collective-permute-start.19 = (s16[272,128]{1,0:T(8,128)(2,1)S(1)}, s16[272,128]{1,0:T(8,128)(2,1)S(1)}, u32[]{:S(2)}, u32[]{:S(2)}) collective-permute-start(s16[272,128]{1,0:T(8,128)(2,1)S(1)} %get-tuple-element.70), channel_id=1, source_target_pairs={{0,4},{1,5},{2,6},{3,7},{4,8},{5,9},{6,10},{7,11},{8,12},{9,13},{1... | collective-permute-start | bytes 208904 | tf_op jit(solution)/shard_map/ppermute | solution.py:387
  74.9 7.3 %collective-permute-start.20 = (s16[272,128]{1,0:T(8,128)(2,1)S(1)}, s16[272,128]{1,0:T(8,128)(2,1)S(1)}, u32[]{:S(2)}, u32[]{:S(2)}) collective-permute-start(s16[272,128]{1,0:T(8,128)(2,1)S(1)} %get-tuple-element.71), channel_id=1, source_target_pairs={{0,8},{1,9},{2,10},{3,11},{4,12},{5,13},{6,14},{7,15},{8,0},{9,1},... | collective-permute-start | bytes 208904 | tf_op jit(solution)/shard_map/ppermute | solution.py:387
  78.1 4.3 %collective-permute-start.21 = (s16[272,128]{1,0:T(8,128)(2,1)S(1)}, s16[272,128]{1,0:T(8,128)(2,1)S(1)}, u32[]{:S(2)}, u32[]{:S(2)}) collective-permute-start(s16[272,128]{1,0:T(8,128)(2,1)S(1)} %get-tuple-element.72), channel_id=1, source_target_pairs={{0,12},{1,13},{2,14},{3,15},{4,0},{5,1},{6,2},{7,3},{8,4},{9,5},{1... | collective-permute-start | bytes 208904 | tf_op jit(solution)/shard_map/ppermute | solution.py:387
  (2 other events, 12.1 us)
